TPU v7x, 512 devices: a whole 4x8x8 slice. The times are simulated.
512 devices in a mesh: gz: 32 (over y_hi, z), gy: 8 (over y_lo, x), gx: 2 (over core).
Axes of the slice: x: 4, y: 8 (y_hi: 4, y_lo: 2; y = y_hi * 2 + y_lo), z: 8, core: 2. Of those that a mesh axis runs over, the one named last changes fastest.
Arguments:
- tokens: bfloat16 [128, 64, 32, 192], P('gz', 'gy', 'gx'), may hold values from -4.5 to 4.5
- layer_norm_gain: float32 [192], replicated, may hold values from 0.25 to 1.75
- layer_norm_bias: float32 [192], replicated, may hold values from -3 to 3
- qkv_weight: bfloat16 [192, 576], replicated, may hold values from -3 to 3
- qkv_bias: float32 [576], replicated, may hold values from -3 to 3
- proj_weight: bfloat16 [192, 192], replicated, may hold values from -0.4375 to 0.4375
- bias_table: float32 [6, 1575], replicated, may hold values from -4 to 4
- grad_out: bfloat16 [128, 64, 32, 192], P('gz', 'gy', 'gx'), may hold values from -9 to 9
Outputs:
- grad_tokens: bfloat16 [128, 64, 32, 192], P('gz', 'gy', 'gx')
- grad_ln_gain: float32 [192], replicated
- grad_ln_shift: float32 [192], replicated
- grad_qkv_weight: float32 [192, 576], replicated
- grad_qkv_bias: float32 [576], replicated
- grad_proj_weight: float32 [192, 192], replicated
- grad_table: float32 [6, 1575], replicated
All inputs are finite; a program needn't handle non-finite values.
Results may differ from a plain program's by a relative error of at most 0.019.
The roundings to bfloat16 on the way count: a program that leaves them out, or rounds other values in their place, can miss the bound.
Values may be sent and summed in bfloat16 or wider, within the bound.
No kernel may reach another device: no remote copies, remote signals or barrier semaphores. Data moves between devices by JAX's collectives and lax.ppermute only.
A program may use at most 128 MiB of HBM per device.

v0:
```python
import math

import jax
import jax.numpy as jnp
from jax import lax
from jax.sharding import PartitionSpec as P

C = 192
HEADS = 6
HD = 32
WZ = 4
WY = 8
WX = 8
SZ = 2
SY = 4
SX = 4
WT = 256
TABLE = 1575


EPSILON = 1e-05
MASKED = -100.0


def shifted(value, axis, steps):
    count = lax.axis_size(axis)
    pairs = [(source, (source + steps) % count) for source in range(count)]
    return lax.ppermute(value, axis, pairs)


def offset_table(width):
    position = jnp.arange(width, dtype=jnp.int32)
    offset = position[:, None] - position[None, :] + width - 1
    slots = jnp.arange(2 * width - 1, dtype=jnp.int32)
    return (offset[:, :, None] == slots[None, None, :]).astype(jnp.float32)


def expand_table(bias_table, depth_table, row_table, col_table):
    exact = lax.Precision.HIGHEST
    table = bias_table.reshape(HEADS, 2 * WZ - 1, 2 * WY - 1, 2 * WX - 1)
    section = jnp.einsum("habc,mnc->habmn", table, col_table, precision=exact)
    section = jnp.einsum("habmn,klb->hakmln", section, row_table, precision=exact)
    section = jnp.einsum("hakmln,ija->hikmjln", section, depth_table, precision=exact)
    return section.reshape(HEADS, WT, WT)


def collect_table(pair_sums, depth_table, row_table, col_table):
    exact = lax.Precision.HIGHEST
    section = pair_sums.reshape(HEADS, WZ, WY, WX, WZ, WY, WX)
    section = jnp.einsum("hikmjln,ija->hakmln", section, depth_table, precision=exact)
    section = jnp.einsum("hakmln,klb->habmn", section, row_table, precision=exact)
    section = jnp.einsum("habmn,mnc->habc", section, col_table, precision=exact)
    return section.reshape(HEADS, TABLE)


def windows_of(field):
    depth, rows, cols = field.shape[:3]
    rest = field.shape[3:]
    field = field.reshape((depth // WZ, WZ, rows // WY, WY, cols // WX, WX) + rest)
    order = (0, 2, 4, 1, 3, 5) + tuple(range(6, 6 + len(rest)))
    return field.transpose(order).reshape((-1, WT) + rest)


def grid_of(windows, depth, rows, cols):
    rest = windows.shape[2:]
    field = windows.reshape((depth // WZ, rows // WY, cols // WX, WZ, WY, WX) + rest)
    order = (0, 3, 1, 4, 2, 5) + tuple(range(6, 6 + len(rest)))
    return field.transpose(order).reshape((depth, rows, cols) + rest)


def apply_layer_norm(field, gain_vector, bias_vector):
    value_rows = field.astype(jnp.float32)
    centered_values = jnp.mean(value_rows, -1, keepdims=True)
    spread = jnp.mean((value_rows - centered_values) ** 2, -1, keepdims=True)
    reciprocal_deviation = lax.rsqrt(spread + EPSILON)
    standardized_input = (value_rows - centered_values) * reciprocal_deviation
    return (
        (standardized_input * gain_vector + bias_vector).astype(jnp.bfloat16),
        standardized_input,
        reciprocal_deviation,
    )


def norm_backward_step(normed_gradient, standardized_input, reciprocal_deviation, gain_vector):
    standardized_gradient = normed_gradient * gain_vector
    first_term = jnp.mean(standardized_gradient, -1, keepdims=True)
    second_term = jnp.mean(standardized_gradient * standardized_input, -1, keepdims=True)
    return reciprocal_deviation * (
        standardized_gradient - first_term - standardized_input * second_term
    )


def region_along(position, count, devices_along, width, half):
    coord = position * count + jnp.arange(count, dtype=jnp.int32)
    total = count * devices_along
    return (coord >= total - width).astype(jnp.int32) + (coord >= total - half).astype(jnp.int32)


def shift_pair(stacked):
    border = stacked[:, :SZ]
    arrived = shifted(border, "gz", -1)
    stacked = jnp.concatenate([stacked[:, SZ:], arrived], 1)
    border = stacked[:, :, :SY]
    arrived = shifted(border, "gy", -1)
    stacked = jnp.concatenate([stacked[:, :, SY:], arrived], 2)
    border = stacked[:, :, :, :SX]
    arrived = shifted(border, "gx", -1)
    return jnp.concatenate([stacked[:, :, :, SX:], arrived], 3)


def unshift_values(field):
    border = field[:, :, -SX:]
    arrived = shifted(border, "gx", 1)
    field = jnp.concatenate([arrived, field[:, :, :-SX]], 2)
    border = field[:, -SY:]
    arrived = shifted(border, "gy", 1)
    field = jnp.concatenate([arrived, field[:, :-SY]], 1)
    border = field[-SZ:]
    arrived = shifted(border, "gz", 1)
    return jnp.concatenate([arrived, field[:-SZ]], 0)


def window_backward(normed_w, cot_w, region_w, qkv_weight, qkv_bias, proj_weight, bias_full):
    groups = normed_w.shape[0]
    factor = HD ** (-0.5)
    f32 = jnp.float32
    flat_normed = normed_w.reshape(-1, C)
    qkv = (jnp.dot(flat_normed, qkv_weight, preferred_element_type=f32) + qkv_bias).astype(
        jnp.bfloat16
    )
    qkv = qkv.reshape(groups, WT, 3, HEADS, HD).transpose(2, 0, 3, 1, 4)
    query, keys_all, value_rows = (qkv[0], qkv[1], qkv[2])
    shared = region_w[:, :, None] == region_w[:, None, :]
    penalty = jnp.where(shared, 0.0, MASKED).astype(f32)[:, None]
    scores = jnp.einsum("ghqd,ghkd->ghqk", query, keys_all, preferred_element_type=f32) * factor
    scores = scores + bias_full[None] + penalty
    highest = jnp.max(scores, -1, keepdims=True)
    exponent = jnp.exp(scores - highest)
    probs = exponent / jnp.sum(exponent, -1, keepdims=True)
    probs_b = probs.astype(jnp.bfloat16)
    attended = jnp.einsum(
        "ghqk,ghkd->ghqd", probs_b, value_rows, preferred_element_type=f32
    ).astype(jnp.bfloat16)
    attended = attended.transpose(0, 2, 1, 3).reshape(-1, C)
    flat_cot = cot_w.reshape(-1, C)
    grad_proj = lax.dot_general(
        attended, flat_cot, (((0,), (0,)), ((), ())), preferred_element_type=f32
    )
    d_att = jnp.dot(flat_cot, proj_weight.T, preferred_element_type=f32).astype(jnp.bfloat16)
    d_att = d_att.reshape(groups, WT, HEADS, HD).transpose(0, 2, 1, 3)
    d_probs = jnp.einsum("ghqd,ghkd->ghqk", d_att, value_rows, preferred_element_type=f32)
    d_values = jnp.einsum("ghqk,ghqd->ghkd", probs_b, d_att, preferred_element_type=f32).astype(
        jnp.bfloat16
    )
    d_scores = probs * (d_probs - jnp.sum(probs * d_probs, -1, keepdims=True))
    d_scores_b = d_scores.astype(jnp.bfloat16)
    d_query = (
        jnp.einsum("ghqk,ghkd->ghqd", d_scores_b, keys_all, preferred_element_type=f32) * factor
    ).astype(jnp.bfloat16)
    d_keys = (
        jnp.einsum("ghqk,ghqd->ghkd", d_scores_b, query, preferred_element_type=f32) * factor
    ).astype(jnp.bfloat16)
    d_qkv = jnp.stack([d_query, d_keys, d_values], 0).transpose(1, 3, 0, 2, 4).reshape(-1, 3 * C)
    grad_qkv = lax.dot_general(
        flat_normed, d_qkv, (((0,), (0,)), ((), ())), preferred_element_type=f32
    )
    grad_qkv_b = jnp.sum(d_qkv.astype(f32), 0)
    normed_gradient = jnp.dot(d_qkv, qkv_weight.T, preferred_element_type=f32).reshape(
        groups, WT, C
    )
    return (normed_gradient, grad_proj, grad_qkv, grad_qkv_b, jnp.sum(d_scores, 0))


def per_device(
    tokens,
    layer_norm_gain,
    layer_norm_bias,
    qkv_weight,
    qkv_bias,
    proj_weight,
    bias_table,
    grad_out,
):
    f32 = jnp.float32
    depth, rows, cols = tokens.shape[:3]
    normed_tokens, standardized_input, reciprocal_deviation = apply_layer_norm(
        tokens, layer_norm_gain, layer_norm_bias
    )
    moved = shift_pair(jnp.stack([normed_tokens, grad_out], 0))
    normed_tokens = moved[0]
    shifted_cot = moved[1]
    region_z = region_along(lax.axis_index("gz"), depth, lax.axis_size("gz"), WZ, SZ)
    region_y = region_along(lax.axis_index("gy"), rows, lax.axis_size("gy"), WY, SY)
    region_x = region_along(lax.axis_index("gx"), cols, lax.axis_size("gx"), WX, SX)
    region = region_z[:, None, None] * 9 + region_y[None, :, None] * 3 + region_x[None, None, :]
    normed_w = windows_of(normed_tokens)
    cot_w = windows_of(shifted_cot)
    region_w = windows_of(region)
    windows = normed_w.shape[0]
    per_step = math.gcd(windows, max(1, 512 // WT))
    steps_count = windows // per_step
    depth_table = offset_table(WZ)
    row_table = offset_table(WY)
    col_table = offset_table(WX)
    bias_full = expand_table(bias_table, depth_table, row_table, col_table)

    def visit(carry, piece):
        result = window_backward(
            piece[0], piece[1], piece[2], qkv_weight, qkv_bias, proj_weight, bias_full
        )
        terms = result[1:]
        return (tuple((a + b for a, b in zip(carry, terms))), result[0])

    init = (
        jnp.zeros((C, C), f32),
        jnp.zeros((C, 3 * C), f32),
        jnp.zeros((3 * C,), f32),
        jnp.zeros((HEADS, WT, WT), f32),
    )
    pieces = (
        normed_w.reshape(steps_count, per_step, WT, C),
        cot_w.reshape(steps_count, per_step, WT, C),
        region_w.reshape(steps_count, per_step, WT),
    )
    sums, d_windows = lax.scan(visit, init, pieces)
    normed_gradient = grid_of(d_windows.reshape(windows, WT, C), depth, rows, cols)
    grad_proj, grad_qkv, grad_qkv_b, pair_sums = sums
    table_part = collect_table(pair_sums, depth_table, row_table, col_table)
    local_gradient = unshift_values(normed_gradient)
    input_gradient = norm_backward_step(
        local_gradient, standardized_input, reciprocal_deviation, layer_norm_gain
    )
    grad_tokens = (grad_out.astype(f32) + input_gradient).astype(jnp.bfloat16)
    gain_product = jnp.sum(local_gradient * standardized_input, (0, 1, 2))
    shift_term = jnp.sum(local_gradient, (0, 1, 2))
    grad_proj, grad_qkv, grad_qkv_b, table_part, gain_product, shift_term = lax.psum(
        (grad_proj, grad_qkv, grad_qkv_b, table_part, gain_product, shift_term), ("gz", "gy", "gx")
    )
    total_tokens = (
        depth * rows * cols * lax.axis_size("gz") * lax.axis_size("gy") * lax.axis_size("gx")
    )
    factor = 1.0 / math.sqrt(total_tokens)
    return (
        grad_tokens,
        gain_product * factor,
        shift_term * factor,
        grad_qkv * factor,
        grad_qkv_b * factor,
        grad_proj * factor,
        table_part * factor,
    )


def solution(mesh):
    placed = (P("gz", "gy", "gx", None), P(), P(), P(), P(), P(), P(), P("gz", "gy", "gx", None))
    return jax.shard_map(
        per_device,
        mesh=mesh,
        in_specs=placed,
        out_specs=(P("gz", "gy", "gx", None), P(), P(), P(), P(), P(), P()),
        check_vma=False,
    )
```

profile of v0, /device:TPU:1, one launch (start us, length us, event | category | flops | bytes accessed | tf_op | source)
XLA Modules:
  0.0 623.1 jit_solution(3815118136035900415)
XLA Ops:
  8.4 1.2 fusion.43
  10.8 1.9 fusion.51
  12.7 15.2 %collective-permute-start = (bf16[2,2,8,16,192]{4,3,2,1,0:T(8,128)(2,1)}, bf16[2,2,8,16,192]{4,3,2,1,0:T(8,128)(2,1)}, u32[]{:S(2)}, u32[]{:S(2)}) collective-permute-start(bf16[2,2,8,16,192]{4,3,2,1,0:T(8,128)(2,1)} %get-tuple-element.67), channel_id=1, source_target_pairs={{0,496},{16,0},{32,16},{48,32},{64,48},{80,64},{96,80},{112,96},{1... | collective-permute-start | bytes 589832 | tf_op jit(solution)/shard_map/ppermute | solution.py:28
  28.9 1.6 convolution_bitcast_fusion.2
  30.5 12.1 %convolution_bitcast_fusion.1 = f32[6,7,8,8,8,8]{5,4,3,1,0,2:T(8,128)S(1)} fusion(f32[6,7,15,8,8]{2,4,1,0,3:T(8,128)S(1)} %convolution_bitcast_fusion.2, s32[8,8]{1,0:T(8,128)S(1)} %subtract_add_fusion), kind=kOutput, calls=%fused_computation.8 | convolution fusion | flops 30966720 | bytes 849664 | tf_op jit(solution)/shard_map/habmn,klb->hakmln/dot_general | solution.py:42
  42.7 22.5 %fusion.6 = f32[6,4,8,8,4,8,8]{6,4,5,3,2,0,1:T(4,128)} fusion(f32[6,7,8,8,8,8]{5,4,3,1,0,2:T(8,128)S(1)} %convolution_bitcast_fusion.1, s32[4,4]{1,0:T(4,128)S(1)} %subtract_add_fusion.1), kind=kOutput, calls=%fused_computation.6 | convolution fusion | flops 33030256 | bytes 2261056 | tf_op jit(solution)/shard_map/hakmln,ija->hikmjln/dot_general | solution.py:43
  65.2 32.0 %copy.67 = f32[6,4,8,8,4,8,8]{3,2,1,6,5,4,0:T(8,128)} copy(f32[6,4,8,8,4,8,8]{6,4,5,3,2,0,1:T(4,128)} %fusion.6) | data formatting | bytes 3145728 | tf_op jit(solution)/shard_map/while/body/eval_jaxpr/add | solution.py:136
  97.2 19.4 %reshape.217 = f32[6,256,256]{1,2,0:T(8,128)} reshape(f32[6,4,8,8,4,8,8]{3,2,1,6,5,4,0:T(8,128)} %copy.67) | data formatting | bytes 3145728 | tf_op jit(solution)/shard_map/while/body/eval_jaxpr/add | solution.py:136
  118.8 4.5 collective-permute-start.1
  123.4 4.6 collective-permute-done.1
  128.1 4.1 collective-permute-start.2
  137.0 3.0 fusion.85
  140.1 2.1 fusion.24
  142.8 2.1 fusion.19
  147.4 1.4 copy.48
  148.8 3.2 copy.46
  155.0 2.1 fusion.86
  157.2 17.1 %reshape.204 = f32[6,4,8,8,4,8,8]{3,2,1,6,5,4,0:T(8,128)} reshape(f32[6,256,256]{1,2,0:T(8,128)} %get-tuple-element.57) | data formatting | bytes 3145728 | tf_op jit(solution)/shard_map/reshape | solution.py:49
  174.2 32.2 %copy.51 = f32[6,4,8,8,4,8,8]{6,4,1,5,3,2,0:T(4,128)} copy(f32[6,4,8,8,4,8,8]{3,2,1,6,5,4,0:T(8,128)} %reshape.204) | data formatting | bytes 3145728 | tf_op jit(solution)/shard_map/reshape | solution.py:49
  206.4 21.0 %convolution_bitcast_fusion = f32[6,7,8,8,8,8]{5,1,4,3,2,0:T(8,128)S(1)} fusion(f32[6,4,8,8,4,8,8]{6,4,1,5,3,2,0:T(4,128)} %copy.51, pred[4,4,7,1,1,1,1]{2,1,0,6,5,4,3:T(4,128)(4,1)S(1)} %fusion.105), kind=kOutput, calls=%fused_computation.7 | convolution fusion | flops 33030144 | bytes 2261104 | tf_op jit(solution)/shard_map/hikmjln,ija->hakmln/dot_general | solution.py:50
  227.4 9.8 %fusion.13 = f32[6,7,15,8,8]{2,4,3,1,0:T(8,128)} fusion(f32[6,7,8,8,8,8]{5,1,4,3,2,0:T(8,128)S(1)} %convolution_bitcast_fusion, s32[8,8]{1,0:T(8,128)S(1)} %subtract_add_fusion), kind=kOutput, calls=%fused_computation.18 | convolution fusion | flops 30966720 | bytes 849664 | tf_op jit(solution)/shard_map/hakmln,klb->habmn/dot_general | solution.py:51
  237.2 2.5 reshape.200
  239.7 1.6 convolution_bitcast_fusion.3
  241.4 2.3 collective-permute-start.3
  243.7 1.3 convolution_bitcast_fusion.4
  245.3 2.9 collective-permute-start.4
  249.1 9.1 %collective-permute-done.4 = f32[4,4,16,192]{3,2,1,0:T(8,128)S(1)} collective-permute-done((f32[4,4,16,192]{3,2,1,0:T(8,128)S(1)}, f32[4,4,16,192]{3,2,1,0:T(8,128)S(1)}, u32[]{:S(2)}, u32[]{:S(2)}) %collective-permute-start.4) | collective-permute-done | bytes 196640 | tf_op jit(solution)/shard_map/ppermute | solution.py:28
  258.3 1.9 collective-permute-start.5
  260.2 253.9 %all-reduce.4.cloned.1.call-done = (f32[192,576]{1,0:T(8,128)}, f32[192,192]{1,0:T(8,128)}) async-done(((f32[192,576]{1,0:T(8,128)}, f32[192,192]{1,0:T(8,128)}), (f32[192,576]{1,0:T(8,128)}, f32[192,192]{1,0:T(8,128)})) %all-reduce.4.cloned.1.call-update) | async-done | bytes 589840 | tf_op jit(solution)/shard_map/psum | solution.py:236
  514.1 1.8 broadcast_multiply_fusion
  516.0 1.6 broadcast_multiply_fusion.1
  518.1 94.8 %all-reduce = (f32[192]{0:T(256)S(1)}, f32[192]{0:T(256)S(1)}, f32[576]{0:T(1024)S(1)}, f32[6,1575]{1,0:T(8,128)S(1)}) all-reduce(f32[192]{0:T(256)S(1)} %get-tuple-element.33, f32[192]{0:T(256)S(1)} %reduce_sum.113, f32[576]{0:T(1024)S(1)} %reduce_sum.115, ...), channel_id=1, replica_groups=mesh['gz'=32,'gy'=8,'gx'=2] {'gz','gy','gx'}, use_global_device_ids=true, to_apply=%region_8.9 | all-reduce | flops 10410 | bytes 83280 | tf_op jit(solution)/shard_map/psum | solution.py:236
  (86 shorter events, 21.5 us)
Async XLA Ops:
  7.2 126.7 %copy-start = (bf16[192,576]{1,0:T(8,128)(2,1)S(1)}, bf16[192,576]{1,0:T(8,128)(2,1)}, u32[]{:S(2)}) copy-start(bf16[192,576]{1,0:T(8,128)(2,1)} %param.11) | copy-start | bytes 663556
  7.2 507.0 %all-reduce.4.cloned.1.call-start = ((), (), s32[]{:S(2)}) async-start(), calls=%async_computation | async-start | bytes 1376256 | tf_op jit(solution)/shard_map/psum | solution.py:236
  12.7 105.1 %collective-permute-start = (bf16[2,2,8,16,192]{4,3,2,1,0:T(8,128)(2,1)}, bf16[2,2,8,16,192]{4,3,2,1,0:T(8,128)(2,1)}, u32[]{:S(2)}, u32[]{:S(2)}) collective-permute-start(bf16[2,2,8,16,192]{4,3,2,1,0:T(8,128)(2,1)} %get-tuple-element.67), channel_id=1, source_target_pairs={{0,496},{16,0},{32,16},{48,32},{64,48},{80,64},{96,80},{112,96},{1... | collective-permute-start | bytes 589832 | tf_op jit(solution)/shard_map/ppermute | solution.py:28
  97.2 20.6 %copy-start.9 = (bf16[2,2,8,16,192]{4,3,2,1,0:T(8,128)(2,1)S(1)}, bf16[2,2,8,16,192]{4,3,2,1,0:T(8,128)(2,1)}, u32[]{:S(2)}) copy-start(bf16[2,2,8,16,192]{4,3,2,1,0:T(8,128)(2,1)} %get-tuple-element.66) | copy-start | bytes 589828
  116.6 17.3 %copy-start.14 = (f32[576]{0:T(1024)S(1)}, f32[576]{0:T(1024)}, u32[]{:S(2)}) copy-start(f32[576]{0:T(1024)} %param.12) | copy-start | bytes 6916
  118.8 9.1 %collective-permute-start.1 = (bf16[2,4,4,16,192]{4,3,2,1,0:T(8,128)(2,1)S(1)}, bf16[2,4,4,16,192]{4,3,2,1,0:T(8,128)(2,1)S(1)}, u32[]{:S(2)}, u32[]{:S(2)}) collective-permute-start(bf16[2,4,4,16,192]{4,3,2,1,0:T(8,128)(2,1)S(1)} %get-tuple-element.65), channel_id=1, source_target_pairs={{0,14},{2,0},{4,2},{6,4},{8,6},{10,8},{12,10},{14,12},{1,15},{3,1}... | collective-permute-start | bytes 589832 | tf_op jit(solution)/shard_map/ppermute | solution.py:28
  128.0 8.0 %copy-start.12 = (bf16[192,192]{1,0:T(8,128)(2,1)S(1)}, bf16[192,192]{1,0:T(8,128)(2,1)}, u32[]{:S(2)}) copy-start(bf16[192,192]{1,0:T(8,128)(2,1)} %param.13) | copy-start | bytes 221188
  128.1 4.9 collective-permute-start.2
  133.2 0.7 copy-start.7
  135.4 0.7 copy-start.4
  140.1 2.1 copy-start.6
  140.1 2.1 copy-start.11
  146.6 0.8 copy-start.3
  239.7 4.0 copy-start.2
  239.7 8.5 %copy-start.5 = (bf16[1,4,1,8,2,8,192]{6,5,3,1,4,2,0:T(8,128)(2,1)S(1)}, bf16[1,4,1,8,2,8,192]{6,5,3,1,4,2,0:T(8,128)(2,1)}, u32[]{:S(2)}) copy-start(bf16[1,4,1,8,2,8,192]{6,5,3,1,4,2,0:T(8,128)(2,1)} %copy-done.4) | copy-start | bytes 589828
  239.7 8.5 %copy-start.10 = (bf16[24,8,2,256]{3,1,2,0:T(8,128)(2,1)S(1)}, bf16[24,8,2,256]{3,1,2,0:T(8,128)(2,1)}, u32[]{:S(2)}) copy-start(bf16[24,8,2,256]{3,1,2,0:T(8,128)(2,1)} %copy.70) | copy-start | bytes 589828
  241.4 3.8 collective-permute-start.3
  245.2 272.4 %copy-start.1 = (bf16[4,8,16,192]{3,2,1,0:T(8,128)(2,1)S(1)}, bf16[4,8,16,192]{3,2,1,0:T(8,128)(2,1)}, u32[]{:S(2)}) copy-start(bf16[4,8,16,192]{3,2,1,0:T(8,128)(2,1)} %param.8) | copy-start | bytes 589828
  245.2 272.4 %copy-start.13 = (f32[192]{0:T(256)S(1)}, f32[192]{0:T(256)}, u32[]{:S(2)}) copy-start(f32[192]{0:T(256)} %param.9) | copy-start | bytes 2308
  245.3 12.9 %collective-permute-start.4 = (f32[4,4,16,192]{3,2,1,0:T(8,128)S(1)}, f32[4,4,16,192]{3,2,1,0:T(8,128)S(1)}, u32[]{:S(2)}, u32[]{:S(2)}) collective-permute-start(f32[4,4,16,192]{3,2,1,0:T(8,128)S(1)} %fusion.47), channel_id=1, source_target_pairs={{0,2},{2,4},{4,6},{6,8},{8,10},{10,12},{12,14},{14,0},{1,3},{3,5},... | collective-permute-start | bytes 589832 | tf_op jit(solution)/shard_map/ppermute | solution.py:28
  248.2 366.6 %copy-start.8 = (bf16[4,8,16,192]{3,2,1,0:T(8,128)(2,1)S(1)}, bf16[4,8,16,192]{3,2,1,0:T(8,128)(2,1)}, u32[]{:S(2)}) copy-start(bf16[4,8,16,192]{3,2,1,0:T(8,128)(2,1)} %param.15) | copy-start | bytes 589828
  258.3 259.3 %collective-permute-start.5 = (f32[2,8,16,192]{3,2,1,0:T(8,128)S(1)}, f32[2,8,16,192]{3,2,1,0:T(8,128)S(1)}, u32[]{:S(2)}, u32[]{:S(2)}) collective-permute-start(f32[2,8,16,192]{3,2,1,0:T(8,128)S(1)} %get-tuple-element.63), channel_id=1, source_target_pairs={{0,16},{16,32},{32,48},{48,64},{64,80},{80,96},{96,112},{112,128},... | collective-permute-start | bytes 589832 | tf_op jit(solution)/shard_map/ppermute | solution.py:28
Sparse Core Ops, SparseCore 0:
  249.2 264.8 all-reduce.3
where the time goes:
time: 632 us; the launch traced here: 623 us
  waiting for transfers between devices  268 us (42%)
  local copies, waits for them, and re-layouts  116 us (18%)
  blocking collectives  94.8 us (15%)
  matrix products  80.8 us (13%)
  starting transfers between devices  30.9 us (5%)
  other arithmetic  17.3 us (3%)
  between operations  14.9 us (2%)
    psum x1, waiting for transfers between devices, per_device(): lax.psum((grad_proj, grad_qkv, grad_qkv_b, table_part, gain_product, shif...  254 us
    psum x1, blocking collectives, per_device(): lax.psum((grad_proj, grad_qkv, grad_qkv_b, table_part, gain_product, shif...  94.8 us
    add x2, local copies, waits for them, and re-layouts, window_backward(): scores = scores + bias_full[None] + penalty  51.4 us
    reshape x2, local copies, waits for them, and re-layouts, collect_table(): section = pair_sums.reshape(HEADS, WZ, WY, WX, WZ, WY, WX)  49.3 us
    ppermute x6, starting transfers between devices, shifted(): return lax.ppermute(value, axis, pairs)  30.8 us
    dot_general x1, matrix products, expand_table(): jnp.einsum('hakmln,ija->hikmjln', section, depth_table, precision=exact)  22.5 us
    dot_general x1, matrix products, collect_table(): jnp.einsum('hikmjln,ija->hakmln', section, depth_table, precision=exact)  21 us
    ppermute x6, waiting for transfers between devices, shifted(): return lax.ppermute(value, axis, pairs)  14.2 us
  transfers between devices with their start and end apart: 7, of which 4 were waited for; matrix products, arithmetic and copies ran while one was open for 15% of the time, Pallas kernels for 0%

commit v1 on v0

v1 whole, which is shorter than its diff:
```python
import functools
import math

import jax
import jax.numpy as jnp
import numpy as np
from jax import lax
from jax.experimental import pallas as pl
from jax.experimental.pallas import tpu as pltpu
from jax.sharding import Mesh
from jax.sharding import PartitionSpec as P

C = 192
HEADS = 6
HD = 32
WZ, WY, WX = 4, 8, 8
SZ, SY, SX = 2, 4, 4
WT = 256
TABLE = 1575
EPSILON = 1e-05
MASKED = -100.0
FACTOR = HD ** (-0.5)
GZ = ("yh", "z")
AXES = ("yh", "z", "gy", "gx")
ROWS = 1280
TABLE_ROWS = 6 * C
F32 = jnp.float32
BF16 = jnp.bfloat16


def nn(a, b):
    return lax.dot_general(a, b, (((1,), (0,)), ((), ())), preferred_element_type=F32)


def nt(a, b):
    return lax.dot_general(a, b, (((1,), (1,)), ((), ())), preferred_element_type=F32)


def shifted(value, axis, steps):
    count = lax.axis_size(axis)
    pairs = [(source, (source + steps) % count) for source in range(count)]
    return lax.ppermute(value, axis, pairs)


def roll_lanes(value, steps):
    steps %= WT
    return value if steps == 0 else pltpu.roll(value, steps, 1)


def roll_rows_forward(value):
    return pltpu.roll(value, 0, 1, stride=1, stride_axis=0)


def iota(shape, dim):
    return lax.broadcasted_iota(jnp.int32, shape, dim)


def expand_bias(classes, lane):
    row = iota((8, WT), 0)
    z_slot, y_slot, x_slot = lane // 64, lane // 8 % 8, lane % 8
    by_x = {}
    for sz in range(2):
        for sy in range(2):
            at = sz * 4 + sy * 2
            below = jnp.broadcast_to(roll_lanes(classes[at : at + 1], -8), (8, WT))
            above = jnp.broadcast_to(classes[at + 1 : at + 2], (8, WT))
            by_x[sz, sy] = jnp.where(
                x_slot >= row, roll_rows_forward(above), roll_rows_forward(below)
            )
    parts = []
    for zk in range(WZ):
        by_z = [
            roll_lanes(jnp.where(z_slot < WZ - zk, by_x[1, sy], by_x[0, sy]), 64 * zk)
            for sy in range(2)
        ]
        below = roll_lanes(by_z[0], -64)
        for yk in range(WY):
            parts.append(roll_lanes(jnp.where(y_slot < WY - yk, by_z[1], below), 8 * yk))
    return jnp.concatenate(parts, 0)


def collect_bias(pair_sums, lane):
    row = iota((8, WT), 0)
    z_slot, y_slot, x_slot = lane // 64, lane // 8 % 8, lane % 8
    by_z = [[None, None], [None, None]]
    for zk in range(WZ):
        above = below = None
        for yk in range(WY):
            at = (zk * WY + yk) * WX
            part = roll_lanes(pair_sums[at : at + 8], -8 * yk)
            stays = y_slot < WY - yk
            up = jnp.where(stays, part, 0.0)
            above = up if above is None else above + up
            if yk:
                down = jnp.where(stays, 0.0, part)
                below = down if below is None else below + down
        below = roll_lanes(below, 64)
        stays = z_slot < WZ - zk
        for sy, value in enumerate((below, above)):
            value = roll_lanes(value, -64 * zk)
            for sz, term in enumerate((jnp.where(stays, 0.0, value), jnp.where(stays, value, 0.0))):
                old = by_z[sz][sy]
                by_z[sz][sy] = term if old is None else old + term
    out = []
    for sz in range(2):
        for sy in range(2):
            value = by_z[sz][sy]
            turned = value
            for xk in range(1, WX):
                turned = jnp.where(row == xk, roll_lanes(value, -xk), turned)
            stays = x_slot < WX - row
            out.append(roll_lanes(jnp.sum(jnp.where(stays, 0.0, turned), 0, keepdims=True), 8))
            out.append(jnp.sum(jnp.where(stays, turned, 0.0), 0, keepdims=True))
    return jnp.concatenate(out, 0)


def quadrants(own, y_part, z_part, zy_part, at):
    near, far = (
        jnp.concatenate([ref[:, :, at : at + 8, :].astype(F32) for ref in pair], 1)
        for pair in ((own, y_part), (z_part, zy_part))
    )
    return jnp.concatenate([near, far], 0).reshape(WT, C)


def kernel(
    scale,
    flags_ref,
    own_ref,
    y_ref,
    z_ref,
    zy_ref,
    gain_ref,
    beta_ref,
    w_ref,
    wt_ref,
    qkv_bias_ref,
    qkv_bias_t_ref,
    proj_ref,
    table_ref,
    own_grad_ref,
    y_grad_ref,
    z_grad_ref,
    zy_grad_ref,
    sums_ref,
    xhat_s,
    rstd_s,
    normed_s,
    cot_s,
    qkv_s,
    qkvt_s,
    datt_s,
    dattt_s,
    attt_s,
    dqt_s,
    dkv_s,
    pen_s,
    table_s,
):
    gain = gain_ref[...]
    beta = beta_ref[...]
    lane = iota((8, WT), 1)
    lane_row = iota((1, WT), 1)
    sub_col = iota((WT, 1), 0)

    for w in range(2):
        parts = (own_ref, y_ref, z_ref, zy_ref)
        tok = quadrants(*(ref.at[0] for ref in parts), 8 * w)
        cot = quadrants(*(ref.at[1] for ref in parts), 8 * w).astype(BF16)
        mean = jnp.mean(tok, -1, keepdims=True)
        centred = tok - mean
        rstd = lax.rsqrt(jnp.mean(centred * centred, -1, keepdims=True) + EPSILON)
        xhat = centred * rstd
        normed = (xhat * gain + beta).astype(BF16)
        xhat_s[w] = xhat
        rstd_s[w] = rstd
        normed_s[w] = normed
        cot_s[w] = cot
        for p in range(3):
            qkv_s[w, p] = (nn(normed, w_ref[p]) + qkv_bias_ref[p]).astype(BF16)
            qkvt_s[w, p] = (nt(wt_ref[p], normed) + qkv_bias_t_ref[p]).astype(BF16)
        datt_s[w] = nt(cot, proj_ref[...]).astype(BF16)
        dattt_s[w] = nt(proj_ref[...], cot).astype(BF16)

        fz, fy = flags_ref[0], flags_ref[1]
        fx = flags_ref[2] if w else 0

        def code(t):
            half = (t // 128) * fz * 4 + (t // 32 % 2) * fy * 2
            return half + (t // 4 % 2) * fx if w else half

        pen_s[w] = jnp.where(code(sub_col) == code(lane_row), 0.0, MASKED).astype(F32)

    for h in range(HEADS):
        bias = expand_bias(table_ref[h], lane)
        pair_sums = None
        part = slice(HD * h, HD * h + HD)
        for w in range(2):
            query, keys, values = (qkv_s[w, p, :, part] for p in range(3))
            query_t, keys_t, values_t = (qkvt_s[w, p, part, :] for p in range(3))
            d_att = datt_s[w, :, part]
            d_att_t = dattt_s[w, part, :]
            scores = nn(keys, query_t) * FACTOR + bias + pen_s[w]
            exponent = jnp.exp(scores - jnp.max(scores, 0, keepdims=True))
            probs = exponent * (1.0 / jnp.sum(exponent, 0, keepdims=True))
            probs_b = probs.astype(BF16)
            attt_s[w, part, :] = nn(values_t, probs_b).astype(BF16)
            d_probs = nn(values, d_att_t)
            dkv_s[w, 1, :, part] = nn(probs_b, d_att).astype(BF16)
            d_scores = probs * (d_probs - jnp.sum(probs * d_probs, 0, keepdims=True))
            d_scores_b = d_scores.astype(BF16)
            dqt_s[w, part, :] = nn(keys_t, d_scores_b) * FACTOR
            dkv_s[w, 0, :, part] = (nn(d_scores_b, query) * FACTOR).astype(BF16)
            pair_sums = d_scores if pair_sums is None else pair_sums + d_scores
        found = collect_bias(pair_sums, lane)
        for c in range(8):
            table_s[c, h : h + 1, :] = found[c : c + 1]

    totals = [None] * 4
    vectors = [None] * 5

    def add(store, at, term):
        store[at] = term if store[at] is None else store[at] + term

    for w in range(2):
        normed = normed_s[w]
        normed_t = normed.astype(F32).T.astype(BF16)
        cot = cot_s[w]
        d_query = dqt_s[w].T.astype(BF16)
        d_normed = None
        for p, d_part in enumerate((d_query, dkv_s[w, 0], dkv_s[w, 1])):
            add(totals, p, nn(normed_t, d_part))
            add(vectors, p, jnp.sum(d_part.astype(F32), 0, keepdims=True))
            term = nn(d_part, wt_ref[p])
            d_normed = term if d_normed is None else d_normed + term
        add(totals, 3, nn(attt_s[w], cot))
        xhat = xhat_s[w]
        add(vectors, 3, jnp.sum(d_normed * xhat, 0, keepdims=True))
        add(vectors, 4, jnp.sum(d_normed, 0, keepdims=True))
        d_xhat = d_normed * gain
        first = jnp.mean(d_xhat, -1, keepdims=True)
        second = jnp.mean(d_xhat * xhat, -1, keepdims=True)
        grad = cot.astype(F32) + rstd_s[w] * (d_xhat - first - xhat * second)
        grad = grad.reshape(WZ, WY, 8, C).astype(BF16)
        cols = slice(8 * w, 8 * w + 8)
        own_grad_ref[:, :, cols, :] = grad[:SZ, :SY]
        y_grad_ref[:, :, cols, :] = grad[:SZ, SY:]
        z_grad_ref[:, :, cols, :] = grad[SZ:, :SY]
        zy_grad_ref[:, :, cols, :] = grad[SZ:, SY:]

    for p in range(4):
        sums_ref[C * p : C * p + C, :] = totals[p][:, :128] * scale
    for p in range(2):
        rest = [totals[2 * p][:, 128:], totals[2 * p + 1][:, 128:]]
        sums_ref[C * (4 + p) : C * (5 + p), :] = jnp.concatenate(rest, 1) * scale
    for c in range(8):
        table_s[c, 6:, :] = jnp.zeros((2, WT), F32)
        if c < 5:
            table_s[c, 6:7, :C] = vectors[c]
        sums_ref[TABLE_ROWS + 16 * c : TABLE_ROWS + 16 * c + 8, :] = table_s[c, :, :128] * scale
        sums_ref[TABLE_ROWS + 16 * c + 8 : TABLE_ROWS + 16 * c + 16, :] = table_s[c, :, 128:] * scale


def finish_kernel(sums_ref, qkv_ref, proj_ref, vectors_ref, table_ref):
    firsts = [sums_ref[C * p : C * p + C, :] for p in range(4)]
    rests = [sums_ref[C * (4 + p) : C * (5 + p), :] for p in range(2)]
    parts = []
    for p in range(4):
        rest = rests[p // 2]
        parts += [firsts[p], rest[:, :64] if p % 2 == 0 else rest[:, 64:]]
    qkv_ref[...] = jnp.concatenate(parts[:6], 1)
    proj_ref[...] = jnp.concatenate(parts[6:], 1)
    classes = []
    for c in range(8):
        at = TABLE_ROWS + 16 * c
        classes.append(jnp.concatenate([sums_ref[at : at + 8, :], sums_ref[at + 8 : at + 16, :]], 1))
    for c in range(5):
        vectors_ref[c : c + 1, :] = classes[c][6:7, :C]
    block = iota((8, WT), 1) // 64
    rows = []
    for index in range(1, 2 * WZ):
        sz, z = index // WZ, index % WZ
        joined = None
        for j in range(4):
            term = roll_lanes(classes[4 * sz + j], 64 * (j - z))
            joined = term if joined is None else jnp.where(block == j, term, joined)
        rows.append(joined)
    source = iota((WT, WT), 0)
    dy = source // 8 % 8 + (source // 128) * 8 - 8
    dx = source % 8 + (source // 64 % 2) * 8 - 8
    target = jnp.where((dy > -8) & (dx > -8), (dy + 7) * 15 + dx + 7, -1)
    pick = (target == iota((WT, WT), 1)).astype(F32)
    placed = lax.dot_general(
        jnp.concatenate(rows, 0),
        pick,
        (((1,), (0,)), ((), ())),
        precision=lax.Precision.HIGHEST,
        preferred_element_type=F32,
    )
    table_ref[...] = jnp.concatenate(
        [placed[8 * d : 8 * d + HEADS, :225] for d in range(2 * WZ - 1)], 1
    )


def finish(sums):
    vmem = pl.BlockSpec(memory_space=pltpu.VMEM)
    return pl.pallas_call(
        finish_kernel,
        out_shape=(
            jax.ShapeDtypeStruct((C, 3 * C), F32),
            jax.ShapeDtypeStruct((C, C), F32),
            jax.ShapeDtypeStruct((5, C), F32),
            jax.ShapeDtypeStruct((HEADS, TABLE), F32),
        ),
        in_specs=[vmem],
        out_specs=(vmem,) * 4,
        compiler_params=pltpu.CompilerParams(vmem_limit_bytes=16 * 1024 * 1024),
        name="finish",
    )(sums)


def windows(scale, *operands):
    vmem = pl.BlockSpec(memory_space=pltpu.VMEM)
    quarter = jax.ShapeDtypeStruct((SZ, SY, 16, C), BF16)
    return pl.pallas_call(
        functools.partial(kernel, scale),
        out_shape=(quarter,) * 4 + (jax.ShapeDtypeStruct((ROWS, 128), F32),),
        in_specs=[pl.BlockSpec(memory_space=pltpu.SMEM)] + [vmem] * (len(operands) - 1),
        out_specs=(vmem,) * 5,
        scratch_shapes=[
            pltpu.VMEM((2, WT, C), F32),
            pltpu.VMEM((2, WT, 1), F32),
            pltpu.VMEM((2, WT, C), BF16),
            pltpu.VMEM((2, WT, C), BF16),
            pltpu.VMEM((2, 3, WT, C), BF16),
            pltpu.VMEM((2, 3, C, WT), BF16),
            pltpu.VMEM((2, WT, C), BF16),
            pltpu.VMEM((2, C, WT), BF16),
            pltpu.VMEM((2, C, WT), BF16),
            pltpu.VMEM((2, C, WT), F32),
            pltpu.VMEM((2, 2, WT, C), BF16),
            pltpu.VMEM((2, WT, WT), F32),
            pltpu.VMEM((8, 8, WT), F32),
        ],
        compiler_params=pltpu.CompilerParams(vmem_limit_bytes=48 * 1024 * 1024),
        cost_estimate=pl.CostEstimate(
            flops=1_000_000_000, bytes_accessed=3_000_000, transcendentals=800_000
        ),
        name="windows",
    )(*operands)


def sent(value, gz=0, gy=0, gx=0):
    axes, sizes, steps = [], [], []
    for names, step in ((GZ, gz), (("gy",), gy), (("gx",), gx)):
        if step:
            axes += names
            sizes.append(math.prod(lax.axis_size(a) for a in names))
            steps.append(step)
    pairs = []
    for place in np.ndindex(*sizes):
        to = tuple((p + s) % n for p, s, n in zip(place, steps, sizes))
        pairs.append(tuple(int(np.ravel_multi_index(q, sizes)) for q in (place, to)))
    return lax.ppermute(value, tuple(axes), pairs)


def shift_pair(stacked):
    border = sent(stacked[:, :, :, :SX], gx=-1)
    stacked = jnp.concatenate([stacked[:, :, :, SX:], border], 3)
    y_part = sent(stacked[:, SZ:, :SY], gy=-1)
    z_part = sent(stacked[:, :SZ, SY:], gz=-1)
    zy_part = sent(stacked[:, :SZ, :SY], gz=-1, gy=-1)
    return stacked[:, SZ:, SY:], y_part, z_part, zy_part


def unshift_quarters(own, y_part, z_part, zy_part):
    y_part = sent(y_part, gy=1)
    z_part = sent(z_part, gz=1)
    zy_part = sent(zy_part, gz=1, gy=1)
    near = jnp.concatenate([zy_part, z_part], 1)
    far = jnp.concatenate([y_part, own], 1)
    field = jnp.concatenate([near, far], 0)
    border = sent(field[:, :, -SX:], gx=1)
    return jnp.concatenate([border, field[:, :, :-SX]], 2)


def classes_of(bias_table):
    table = bias_table.reshape(HEADS, 2 * WZ - 1, 2 * WY - 1, 2 * WX - 1)
    table = jnp.pad(table, ((0, 0), (1, 0), (1, 0), (1, 0)))
    table = table.reshape(HEADS, 2, WZ, 2, WY, 2, WX)
    return table.transpose(0, 1, 3, 5, 2, 4, 6).reshape(HEADS, 8, WT)


def swapped(value, axis, partners):
    return lax.ppermute(value, axis, list(enumerate(partners)))


def to_each(value, axis):
    count = lax.axis_size(axis)
    spread = jnp.broadcast_to(value[None], (count,) + value.shape)
    return lax.all_to_all(spread, axis, 0, 0, tiled=True)


def reduce_sums(sums):
    half = ROWS // 2
    core = lax.axis_index("gx")
    mine = lax.dynamic_slice_in_dim(sums, core * half, half, 0)
    other = lax.dynamic_slice_in_dim(sums, (1 - core) * half, half, 0)
    mine = mine + swapped(other, "gx", (1, 0))
    count = lax.axis_size("gy")
    part = lax.all_to_all(mine.reshape(count, half // count, 128), "gy", 0, 0, tiled=True).sum(0)
    part = part + swapped(part, "yh", (1, 0, 3, 2))
    part = part + swapped(part, "yh", (3, 2, 1, 0))
    part = to_each(part, "z").sum(0)
    mine = to_each(part, "gy").reshape(half, 128)
    return lax.all_gather(mine, "gx", axis=0, tiled=True)


def per_device(tokens, ln_gain, ln_bias, qkv_weight, qkv_bias, proj_weight, bias_table, grad_out):
    count = tokens.shape[0] * tokens.shape[1] * tokens.shape[2]
    for axis in AXES:
        count *= lax.axis_size(axis)
    quarters = shift_pair(jnp.stack([tokens, grad_out], 0))
    w3 = qkv_weight.reshape(C, 3, C).transpose(1, 0, 2)
    w3t = qkv_weight.T.reshape(3, C, C)
    last = [lax.axis_index(a) == lax.axis_size(a) - 1 for a in AXES]
    flags = jnp.stack([last[0] & last[1], last[2], last[3]]).astype(jnp.int32)
    *grads, sums = windows(
        1.0 / math.sqrt(count),
        flags,
        *quarters,
        ln_gain.reshape(1, C),
        ln_bias.reshape(1, C),
        w3,
        w3t,
        qkv_bias.reshape(3, 1, C),
        qkv_bias.reshape(3, C, 1),
        proj_weight,
        classes_of(bias_table),
    )
    grad_tokens = unshift_quarters(*grads)
    grad_qkv, grad_proj, vectors, grad_table = finish(reduce_sums(sums))
    return (
        grad_tokens,
        vectors[3],
        vectors[4],
        grad_qkv,
        vectors[:3].reshape(3 * C),
        grad_proj,
        grad_table,
    )


def solution(mesh):
    sizes = mesh.devices.shape
    mesh = Mesh(mesh.devices.reshape(4, sizes[0] // 4, *sizes[1:]), AXES)
    grid = P(GZ, "gy", "gx", None)
    return jax.shard_map(
        per_device,
        mesh=mesh,
        in_specs=(grid, P(), P(), P(), P(), P(), P(), grid),
        out_specs=(grid, P(), P(), P(), P(), P(), P()),
        check_vma=False,
    )
```

time: 632 us -> 124 us (0.20); the launches traced: 623 us -> 123 us
  waiting for transfers between devices: 268 us -> 19.3 us
  local copies, waits for them, and re-layouts: 116 us -> 6.7 us
  matrix products: 80.8 us -> 0 us
  blocking collectives: 94.8 us -> 31.2 us
  starting transfers between devices: 30.9 us -> 53.1 us
  other arithmetic: 17.3 us -> 2.45 us
  between operations: 14.9 us -> 0.93 us
  Pallas kernels: 0 us -> 9.04 us
    psum x1 -> x0, waiting for transfers between devices: 254 us -> none  [per_device(): lax.psum((grad_proj, grad_qkv, grad_qkv_b, table_part, gain_product, shif...]
    psum x1 -> x0, blocking collectives: 94.8 us -> none  [per_device(): lax.psum((grad_proj, grad_qkv, grad_qkv_b, table_part, gain_product, shif...]
    dot_general x16 -> x0, matrix products: 77.8 us -> none  [the longest x1 22.5 us: expand_table(): jnp.einsum('hakmln,ija->hikmjln', section, depth_table, precision=exact)]
    add x2 -> x0, local copies, waits for them, and re-layouts: 51.4 us -> none  [window_backward(): scores = scores + bias_full[None] + penalty]
    reshape x7, local copies, waits for them, and re-layouts: 52.2 us -> 2.18 us  [the longest x1 0.67 us: per_device(): vectors[:3].reshape(3 * C)]
    all_to_all x0 -> x2, blocking collectives: none -> 28.9 us  [the longest x1 16.1 us: to_each(): return lax.all_to_all(spread, axis, 0, 0, tiled=True)]
    ppermute x6 -> x11, starting transfers between devices: 30.8 us -> 49.6 us  [the longest x8 40.5 us: sent(): return lax.ppermute(value, tuple(axes), pairs)]
    pallas_call x0 -> x2, Pallas kernels: none -> 9.04 us  [the longest x1 7.83 us: windows(): pl.pallas_call(functools.partial(kernel, scale), out_shape=(quarter,) * 4...]
  transfers between devices with their start and end apart: 7 -> 12, of which waited for: 4 -> 9; matrix products, arithmetic and copies ran while one was open for 15% -> 3% of each run, Pallas kernels for 0% -> 0%
where the time goes in v1:
time: 124 us; the launch traced here: 123 us
  starting transfers between devices  53.1 us (43%)
  blocking collectives  31.2 us (25%)
  waiting for transfers between devices  19.3 us (16%)
  Pallas kernels  9.04 us (7%)
  local copies, waits for them, and re-layouts  6.7 us (5%)
  other arithmetic  2.45 us (2%)
    ppermute x8, starting transfers between devices, sent(): return lax.ppermute(value, tuple(axes), pairs)  40.5 us
    all_to_all x1, blocking collectives, to_each(): return lax.all_to_all(spread, axis, 0, 0, tiled=True)  16.1 us
    all_to_all x1, blocking collectives, reduce_sums(): lax.all_to_all(mine.reshape(count, half // count, 128), 'gy', 0, 0, tiled...  12.8 us
    ppermute x8, waiting for transfers between devices, sent(): return lax.ppermute(value, tuple(axes), pairs)  10.9 us
    ppermute x3, starting transfers between devices, swapped(): return lax.ppermute(value, axis, list(enumerate(partners)))  9.12 us
    ppermute x3, waiting for transfers between devices, swapped(): return lax.ppermute(value, axis, list(enumerate(partners)))  8.36 us
    pallas_call x1, Pallas kernels, windows(): pl.pallas_call(functools.partial(kernel, scale), out_shape=(quarter,) * 4...  7.83 us
    all_to_all x1, starting transfers between devices, to_each(): return lax.all_to_all(spread, axis, 0, 0, tiled=True)  3.43 us
  transfers between devices with their start and end apart: 12, of which 9 were waited for; matrix products, arithmetic and copies ran while one was open for 3% of the time, Pallas kernels for 0%

profile of v1, /device:TPU:1, one launch (start us, length us, event | category | flops | bytes accessed | tf_op | source)
XLA Modules:
  0.0 122.7 jit_solution(5329071832664079318)
XLA Ops:
  0.6 1.0 pad_maximum_fusion.3
  1.7 8.8 %collective-permute-start = (bf16[2,4,8,4,192]{4,3,2,1,0:T(4,128)(2,1)S(1)}, bf16[2,4,8,4,192]{4,3,2,1,0:T(4,128)(2,1)S(1)}, u32[]{:S(2)}, u32[]{:S(2)}) collective-permute-start(bf16[2,4,8,4,192]{4,3,2,1,0:T(4,128)(2,1)S(1)} %pad_maximum_fusion.3), channel_id=1, source_target_pairs={{0,1},{1,0},{2,3},{3,2},{4,5},{5,4},{6,7},{7,6},{8,9},{9,8},{10,11... | collective-permute-start | bytes 294920 | tf_op jit(solution)/shard_map/ppermute | solution.py:363
  13.7 0.7 copy-done.3
  15.0 1.9 %collective-permute-start.1 = (bf16[2,2,4,16,192]{4,3,2,1,0:T(8,128)(2,1)S(1)}, bf16[2,2,4,16,192]{4,3,2,1,0:T(8,128)(2,1)S(1)}, u32[]{:S(2)}, u32[]{:S(2)}) collective-permute-start(bf16[2,2,4,16,192]{4,3,2,1,0:T(8,128)(2,1)S(1)} %get-tuple-element.27), channel_id=1, source_target_pairs={{0,14},{2,0},{4,2},{6,4},{8,6},{10,8},{12,10},{14,12},{1,15},{3,1}... | collective-permute-start | bytes 294920 | tf_op jit(solution)/shard_map/ppermute | solution.py:363
  16.9 11.6 %collective-permute-start.2 = (bf16[2,2,4,16,192]{4,3,2,1,0:T(8,128)(2,1)S(1)}, bf16[2,2,4,16,192]{4,3,2,1,0:T(8,128)(2,1)S(1)}, u32[]{:S(2)}, u32[]{:S(2)}) collective-permute-start(bf16[2,2,4,16,192]{4,3,2,1,0:T(8,128)(2,1)S(1)} %get-tuple-element.28), channel_id=1, source_target_pairs={{0,496},{16,0},{32,16},{48,32},{64,48},{80,64},{96,80},{112,96},{1... | collective-permute-start | bytes 294920 | tf_op jit(solution)/shard_map/ppermute | solution.py:363
  28.5 1.9 %collective-permute-start.3 = (bf16[2,2,4,16,192]{4,3,2,1,0:T(8,128)(2,1)S(1)}, bf16[2,2,4,16,192]{4,3,2,1,0:T(8,128)(2,1)S(1)}, u32[]{:S(2)}, u32[]{:S(2)}) collective-permute-start(bf16[2,2,4,16,192]{4,3,2,1,0:T(8,128)(2,1)S(1)} %get-tuple-element.25), channel_id=1, source_target_pairs={{0,510},{2,496},{4,498},{6,500},{8,502},{10,504},{12,506},{14,508}... | collective-permute-start | bytes 294920 | tf_op jit(solution)/shard_map/ppermute | solution.py:363
  30.5 1.5 %collective-permute-done.2.z_ref = bf16[2,2,4,16,192]{4,3,2,1,0:T(8,128)(2,1)S(1)} collective-permute-done((bf16[2,2,4,16,192]{4,3,2,1,0:T(8,128)(2,1)S(1)}, bf16[2,2,4,16,192]{4,3,2,1,0:T(8,128)(2,1)S(1)}, u32[]{:S(2)}, u32[]{:S(2)}) %collective-permute-start.2) | collective-permute-done | bytes 98336 | tf_op jit(solution)/shard_map/ppermute | solution.py:363
  32.1 3.7 %collective-permute-done.3.zy_ref = bf16[2,2,4,16,192]{4,3,2,1,0:T(8,128)(2,1)S(1)} collective-permute-done((bf16[2,2,4,16,192]{4,3,2,1,0:T(8,128)(2,1)S(1)}, bf16[2,2,4,16,192]{4,3,2,1,0:T(8,128)(2,1)S(1)}, u32[]{:S(2)}, u32[]{:S(2)}) %collective-permute-start.3) | collective-permute-done | bytes 98336 | tf_op jit(solution)/shard_map/ppermute | solution.py:363
  35.8 0.7 copy-done.1
  36.5 7.8 %windows.1 = (bf16[2,4,16,192]{3,2,1,0:T(8,128)(2,1)S(1)}, bf16[2,4,16,192]{3,2,1,0:T(8,128)(2,1)S(1)}, bf16[2,4,16,192]{3,2,1,0:T(8,128)(2,1)S(1)}, bf16[2,4,16,192]{3,2,1,0:T(8,128)(2,1)S(1)}, f32[1280,128]{1,0:T(8,128)S(1)}) custom-call(s32[3]{0:T(128)S(1)} %add_convert_fusion.flags_ref, bf16[2,2,4,16,192]{4,3,2,1,0:T(8,128)(2,1)S(1)} %get-tuple-element.26.own_ref, ...), custom_call_target="tpu_custom_call" | custom-call | flops 1000000000 | bytes 3000000 | tf_op jit(solution)/shard_map/windows/pallas_call | solution.py:324
  44.3 3.3 %collective-permute-start.8 = (f32[640,128]{1,0:T(8,128)S(1)}, f32[640,128]{1,0:T(8,128)S(1)}, u32[]{:S(2)}, u32[]{:S(2)}) collective-permute-start(f32[640,128]{1,0:T(8,128)S(1)} %constant_dynamic-slice_fusion), channel_id=1, source_target_pairs={{0,1},{1,0},{2,3},{3,2},{4,5},{5,4},{6,7},{7,6},{8,9},{9,8},{10,11... | collective-permute-start | bytes 983048 | tf_op jit(solution)/shard_map/ppermute | solution.py:394
  47.7 1.2 %collective-permute-done.8 = f32[640,128]{1,0:T(8,128)S(1)} collective-permute-done((f32[640,128]{1,0:T(8,128)S(1)}, f32[640,128]{1,0:T(8,128)S(1)}, u32[]{:S(2)}, u32[]{:S(2)}) %collective-permute-start.8) | collective-permute-done | bytes 327712 | tf_op jit(solution)/shard_map/ppermute | solution.py:394
  49.0 12.8 %all_to_all.15 = f32[8,80,128]{2,1,0:T(8,128)S(1)} all-to-all(f32[8,80,128]{2,1,0:T(8,128)S(1)} %bitcast.25), channel_id=1, replica_groups=mesh['yh'=4,'z'=8,'gy'=8,'gx'=2] {'gy'}, dimensions={0} | all-to-all | bytes 655360 | tf_op jit(solution)/shard_map/all_to_all | solution.py:410
  61.8 1.9 %collective-permute-start.9 = (f32[80,128]{1,0:T(8,128)S(1)}, f32[80,128]{1,0:T(8,128)S(1)}, u32[]{:S(2)}, u32[]{:S(2)}) collective-permute-start(f32[80,128]{1,0:T(8,128)S(1)} %reduce_sum.18), channel_id=1, source_target_pairs={{0,128},{128,0},{256,384},{384,256},{1,129},{129,1},{257,385},{385... | collective-permute-start | bytes 122888 | tf_op jit(solution)/shard_map/ppermute | solution.py:394
  63.7 4.2 %collective-permute-done.9 = f32[80,128]{1,0:T(8,128)S(1)} collective-permute-done((f32[80,128]{1,0:T(8,128)S(1)}, f32[80,128]{1,0:T(8,128)S(1)}, u32[]{:S(2)}, u32[]{:S(2)}) %collective-permute-start.9) | collective-permute-done | bytes 40992 | tf_op jit(solution)/shard_map/ppermute | solution.py:394
  67.9 3.9 %collective-permute-start.10 = (f32[80,128]{1,0:T(8,128)S(1)}, f32[80,128]{1,0:T(8,128)S(1)}, u32[]{:S(2)}, u32[]{:S(2)}) collective-permute-start(f32[80,128]{1,0:T(8,128)S(1)} %add.20), channel_id=1, source_target_pairs={{0,384},{128,256},{256,128},{384,0},{1,385},{129,257},{257,129},{3... | collective-permute-start | bytes 122888 | tf_op jit(solution)/shard_map/ppermute | solution.py:394
  71.7 3.0 %collective-permute-done.10 = f32[80,128]{1,0:T(8,128)S(1)} collective-permute-done((f32[80,128]{1,0:T(8,128)S(1)}, f32[80,128]{1,0:T(8,128)S(1)}, u32[]{:S(2)}, u32[]{:S(2)}) %collective-permute-start.10) | collective-permute-done | bytes 40992 | tf_op jit(solution)/shard_map/ppermute | solution.py:394
  74.7 16.1 %all_to_all.16 = f32[8,80,128]{2,1,0:T(8,128)S(1)} all-to-all(f32[8,80,128]{2,1,0:T(8,128)S(1)} %broadcast_in_dim.4), channel_id=1, replica_groups=mesh['yh'=4,'z'=8,'gy'=8,'gx'=2] {'z'}, dimensions={0} | all-to-all | bytes 655360 | tf_op jit(solution)/shard_map/all_to_all | solution.py:400
  90.9 0.7 broadcast_in_dim.5
  91.6 3.4 %all-to-all-start.2 = ((f32[8,80,128]{2,1,0:T(8,128)}), f32[8,80,128]{2,1,0:T(8,128)S(1)}, u32[]{:S(2)}, u32[]{:S(2)}) async-start(f32[8,80,128]{2,1,0:T(8,128)} %broadcast_in_dim.5), calls=%async_computation.2 | async-start | bytes 655360 | tf_op jit(solution)/shard_map/all_to_all | solution.py:400
  95.1 3.4 %collective-permute-start.4 = (bf16[2,4,16,192]{3,2,1,0:T(8,128)(2,1)S(1)}, bf16[2,4,16,192]{3,2,1,0:T(8,128)(2,1)S(1)}, u32[]{:S(2)}, u32[]{:S(2)}) collective-permute-start(bf16[2,4,16,192]{3,2,1,0:T(8,128)(2,1)S(1)} %get-tuple-element.16), channel_id=1, source_target_pairs={{0,18},{2,20},{4,22},{6,24},{8,26},{10,28},{12,30},{14,16},{16,34}... | collective-permute-start | bytes 147464 | tf_op jit(solution)/shard_map/ppermute | solution.py:363
  98.5 1.9 %collective-permute-start.5 = (bf16[2,4,16,192]{3,2,1,0:T(8,128)(2,1)S(1)}, bf16[2,4,16,192]{3,2,1,0:T(8,128)(2,1)S(1)}, u32[]{:S(2)}, u32[]{:S(2)}) collective-permute-start(bf16[2,4,16,192]{3,2,1,0:T(8,128)(2,1)S(1)} %get-tuple-element.17), channel_id=1, source_target_pairs={{0,16},{16,32},{32,48},{48,64},{64,80},{80,96},{96,112},{112,128},... | collective-permute-start | bytes 147464 | tf_op jit(solution)/shard_map/ppermute | solution.py:363
  100.4 3.1 %collective-permute-start.6 = (bf16[2,4,16,192]{3,2,1,0:T(8,128)(2,1)S(1)}, bf16[2,4,16,192]{3,2,1,0:T(8,128)(2,1)S(1)}, u32[]{:S(2)}, u32[]{:S(2)}) collective-permute-start(bf16[2,4,16,192]{3,2,1,0:T(8,128)(2,1)S(1)} %get-tuple-element.18), channel_id=1, source_target_pairs={{0,2},{2,4},{4,6},{6,8},{8,10},{10,12},{12,14},{14,0},{1,3},{3,5},... | collective-permute-start | bytes 147464 | tf_op jit(solution)/shard_map/ppermute | solution.py:363
  103.5 2.3 %collective-permute-done.4 = bf16[2,4,16,192]{3,2,1,0:T(8,128)(2,1)S(1)} collective-permute-done((bf16[2,4,16,192]{3,2,1,0:T(8,128)(2,1)S(1)}, bf16[2,4,16,192]{3,2,1,0:T(8,128)(2,1)S(1)}, u32[]{:S(2)}, u32[]{:S(2)}) %collective-permute-start.4) | collective-permute-done | bytes 49184 | tf_op jit(solution)/shard_map/ppermute | solution.py:363
  105.8 2.1 %collective-permute-done.5 = bf16[2,4,16,192]{3,2,1,0:T(8,128)(2,1)S(1)} collective-permute-done((bf16[2,4,16,192]{3,2,1,0:T(8,128)(2,1)S(1)}, bf16[2,4,16,192]{3,2,1,0:T(8,128)(2,1)S(1)}, u32[]{:S(2)}, u32[]{:S(2)}) %collective-permute-start.5) | collective-permute-done | bytes 49184 | tf_op jit(solution)/shard_map/ppermute | solution.py:363
  108.3 7.9 %collective-permute-start.7 = (bf16[4,8,4,192]{3,2,1,0:T(4,128)(2,1)S(1)}, bf16[4,8,4,192]{3,2,1,0:T(4,128)(2,1)S(1)}, u32[]{:S(2)}, u32[]{:S(2)}) collective-permute-start(bf16[4,8,4,192]{3,2,1,0:T(4,128)(2,1)S(1)} %maximum_maximum_fusion), channel_id=1, source_target_pairs={{0,1},{1,0},{2,3},{3,2},{4,5},{5,4},{6,7},{7,6},{8,9},{9,8},{10,11... | collective-permute-start | bytes 147464 | tf_op jit(solution)/shard_map/ppermute | solution.py:363
  116.3 0.9 collective-permute-done.7
  117.1 0.8 fusion.1
  118.0 2.3 %all_gather.3.sums_ref = f32[1280,128]{1,0:T(8,128)S(1)} all-gather(f32[640,128]{1,0:T(8,128)S(1)} %bitcast.26), channel_id=1, replica_groups=mesh['yh'=4,'z'=8,'gy'=8,'gx'=2] {'gx'}, dimensions={0}, use_global_device_ids=true | all-gather | bytes 983040 | tf_op jit(solution)/shard_map/all_gather | solution.py:415
  120.2 1.2 finish.1
  121.4 0.6 fusion.5
  122.0 0.7 reshape.63
  (40 shorter events, 4.3 us)
Async XLA Ops:
  1.7 8.8 %copy-start.7 = (f32[576]{0:T(1024)S(1)}, f32[576]{0:T(1024)}, u32[]{:S(2)}) copy-start(f32[576]{0:T(1024)} %param.12) | copy-start | bytes 6916
  1.7 13.1 %collective-permute-start = (bf16[2,4,8,4,192]{4,3,2,1,0:T(4,128)(2,1)S(1)}, bf16[2,4,8,4,192]{4,3,2,1,0:T(4,128)(2,1)S(1)}, u32[]{:S(2)}, u32[]{:S(2)}) collective-permute-start(bf16[2,4,8,4,192]{4,3,2,1,0:T(4,128)(2,1)S(1)} %pad_maximum_fusion.3), channel_id=1, source_target_pairs={{0,1},{1,0},{2,3},{3,2},{4,5},{5,4},{6,7},{7,6},{8,9},{9,8},{10,11... | collective-permute-start | bytes 294920 | tf_op jit(solution)/shard_map/ppermute | solution.py:363
  10.5 0.8 copy-start.6
  12.2 1.0 copy-start.5
  13.5 1.0 copy-start.3
  13.5 1.0 copy-start.4
  14.7 21.1 %copy-start = (bf16[192,192]{1,0:T(8,128)(2,1)S(1)}, bf16[192,192]{1,0:T(8,128)(2,1)}, u32[]{:S(2)}) copy-start(bf16[192,192]{1,0:T(8,128)(2,1)} %proj_ref.1) | copy-start | bytes 221188
  14.7 21.0 %copy-start.2 = (f32[192]{0:T(256)S(1)}, f32[192]{0:T(256)}, u32[]{:S(2)}) copy-start(f32[192]{0:T(256)} %param.10) | copy-start | bytes 2308
  15.0 15.5 %collective-permute-start.1 = (bf16[2,2,4,16,192]{4,3,2,1,0:T(8,128)(2,1)S(1)}, bf16[2,2,4,16,192]{4,3,2,1,0:T(8,128)(2,1)S(1)}, u32[]{:S(2)}, u32[]{:S(2)}) collective-permute-start(bf16[2,2,4,16,192]{4,3,2,1,0:T(8,128)(2,1)S(1)} %get-tuple-element.27), channel_id=1, source_target_pairs={{0,14},{2,0},{4,2},{6,4},{8,6},{10,8},{12,10},{14,12},{1,15},{3,1}... | collective-permute-start | bytes 294920 | tf_op jit(solution)/shard_map/ppermute | solution.py:363
  16.9 15.1 %collective-permute-start.2 = (bf16[2,2,4,16,192]{4,3,2,1,0:T(8,128)(2,1)S(1)}, bf16[2,2,4,16,192]{4,3,2,1,0:T(8,128)(2,1)S(1)}, u32[]{:S(2)}, u32[]{:S(2)}) collective-permute-start(bf16[2,2,4,16,192]{4,3,2,1,0:T(8,128)(2,1)S(1)} %get-tuple-element.28), channel_id=1, source_target_pairs={{0,496},{16,0},{32,16},{48,32},{64,48},{80,64},{96,80},{112,96},{1... | collective-permute-start | bytes 294920 | tf_op jit(solution)/shard_map/ppermute | solution.py:363
  28.5 7.3 %collective-permute-start.3 = (bf16[2,2,4,16,192]{4,3,2,1,0:T(8,128)(2,1)S(1)}, bf16[2,2,4,16,192]{4,3,2,1,0:T(8,128)(2,1)S(1)}, u32[]{:S(2)}, u32[]{:S(2)}) collective-permute-start(bf16[2,2,4,16,192]{4,3,2,1,0:T(8,128)(2,1)S(1)} %get-tuple-element.25), channel_id=1, source_target_pairs={{0,510},{2,496},{4,498},{6,500},{8,502},{10,504},{12,506},{14,508}... | collective-permute-start | bytes 294920 | tf_op jit(solution)/shard_map/ppermute | solution.py:363
  35.8 0.7 copy-start.1
  44.3 4.6 %collective-permute-start.8 = (f32[640,128]{1,0:T(8,128)S(1)}, f32[640,128]{1,0:T(8,128)S(1)}, u32[]{:S(2)}, u32[]{:S(2)}) collective-permute-start(f32[640,128]{1,0:T(8,128)S(1)} %constant_dynamic-slice_fusion), channel_id=1, source_target_pairs={{0,1},{1,0},{2,3},{3,2},{4,5},{5,4},{6,7},{7,6},{8,9},{9,8},{10,11... | collective-permute-start | bytes 983048 | tf_op jit(solution)/shard_map/ppermute | solution.py:394
  61.8 6.1 %collective-permute-start.9 = (f32[80,128]{1,0:T(8,128)S(1)}, f32[80,128]{1,0:T(8,128)S(1)}, u32[]{:S(2)}, u32[]{:S(2)}) collective-permute-start(f32[80,128]{1,0:T(8,128)S(1)} %reduce_sum.18), channel_id=1, source_target_pairs={{0,128},{128,0},{256,384},{384,256},{1,129},{129,1},{257,385},{385... | collective-permute-start | bytes 122888 | tf_op jit(solution)/shard_map/ppermute | solution.py:394
  67.9 6.8 %collective-permute-start.10 = (f32[80,128]{1,0:T(8,128)S(1)}, f32[80,128]{1,0:T(8,128)S(1)}, u32[]{:S(2)}, u32[]{:S(2)}) collective-permute-start(f32[80,128]{1,0:T(8,128)S(1)} %add.20), channel_id=1, source_target_pairs={{0,384},{128,256},{256,128},{384,0},{1,385},{129,257},{257,129},{3... | collective-permute-start | bytes 122888 | tf_op jit(solution)/shard_map/ppermute | solution.py:394
  91.6 26.3 %all-to-all-start.2 = ((f32[8,80,128]{2,1,0:T(8,128)}), f32[8,80,128]{2,1,0:T(8,128)S(1)}, u32[]{:S(2)}, u32[]{:S(2)}) async-start(f32[8,80,128]{2,1,0:T(8,128)} %broadcast_in_dim.5), calls=%async_computation.2 | async-start | bytes 655360 | tf_op jit(solution)/shard_map/all_to_all | solution.py:400
  95.1 10.8 %collective-permute-start.4 = (bf16[2,4,16,192]{3,2,1,0:T(8,128)(2,1)S(1)}, bf16[2,4,16,192]{3,2,1,0:T(8,128)(2,1)S(1)}, u32[]{:S(2)}, u32[]{:S(2)}) collective-permute-start(bf16[2,4,16,192]{3,2,1,0:T(8,128)(2,1)S(1)} %get-tuple-element.16), channel_id=1, source_target_pairs={{0,18},{2,20},{4,22},{6,24},{8,26},{10,28},{12,30},{14,16},{16,34}... | collective-permute-start | bytes 147464 | tf_op jit(solution)/shard_map/ppermute | solution.py:363
  98.5 9.4 %collective-permute-start.5 = (bf16[2,4,16,192]{3,2,1,0:T(8,128)(2,1)S(1)}, bf16[2,4,16,192]{3,2,1,0:T(8,128)(2,1)S(1)}, u32[]{:S(2)}, u32[]{:S(2)}) collective-permute-start(bf16[2,4,16,192]{3,2,1,0:T(8,128)(2,1)S(1)} %get-tuple-element.17), channel_id=1, source_target_pairs={{0,16},{16,32},{32,48},{48,64},{64,80},{80,96},{96,112},{112,128},... | collective-permute-start | bytes 147464 | tf_op jit(solution)/shard_map/ppermute | solution.py:363
  100.4 7.9 %collective-permute-start.6 = (bf16[2,4,16,192]{3,2,1,0:T(8,128)(2,1)S(1)}, bf16[2,4,16,192]{3,2,1,0:T(8,128)(2,1)S(1)}, u32[]{:S(2)}, u32[]{:S(2)}) collective-permute-start(bf16[2,4,16,192]{3,2,1,0:T(8,128)(2,1)S(1)} %get-tuple-element.18), channel_id=1, source_target_pairs={{0,2},{2,4},{4,6},{6,8},{8,10},{10,12},{12,14},{14,0},{1,3},{3,5},... | collective-permute-start | bytes 147464 | tf_op jit(solution)/shard_map/ppermute | solution.py:363
  108.3 8.8 %collective-permute-start.7 = (bf16[4,8,4,192]{3,2,1,0:T(4,128)(2,1)S(1)}, bf16[4,8,4,192]{3,2,1,0:T(4,128)(2,1)S(1)}, u32[]{:S(2)}, u32[]{:S(2)}) collective-permute-start(bf16[4,8,4,192]{3,2,1,0:T(4,128)(2,1)S(1)} %maximum_maximum_fusion), channel_id=1, source_target_pairs={{0,1},{1,0},{2,3},{3,2},{4,5},{5,4},{6,7},{7,6},{8,9},{9,8},{10,11... | collective-permute-start | bytes 147464 | tf_op jit(solution)/shard_map/ppermute | solution.py:363

commit v2 on v1

--- a/solution.py
+++ b/solution.py
@@ -21,9 +21,11 @@
 MASKED = -100.0
 FACTOR = HD ** (-0.5)
 GZ = ("yh", "z")
+PLANE = ("yh", "gy")
 AXES = ("yh", "z", "gy", "gx")
-ROWS = 1280
+ROWS = 1536
 TABLE_ROWS = 6 * C
+USED = TABLE_ROWS + 128
 F32 = jnp.float32
 BF16 = jnp.bfloat16
 
@@ -114,33 +116,48 @@
     return jnp.concatenate(out, 0)
 
 
-def quadrants(own, y_part, z_part, zy_part, at):
+def block_of(own, y_part, z_part, zy_part):
     near, far = (
-        jnp.concatenate([ref[:, :, at : at + 8, :].astype(F32) for ref in pair], 1)
+        jnp.concatenate([ref[...].astype(F32) for ref in pair], 1)
         for pair in ((own, y_part), (z_part, zy_part))
     )
-    return jnp.concatenate([near, far], 0).reshape(WT, C)
+    return jnp.concatenate([near, far], 0).reshape(WZ * WY, 16, 2 * C)
+
+
+def windows_of(block, border):
+    first, second = block[:, :8], block[:, 8:]
+    border = jnp.concatenate([border, border], 1)
+    early = iota((WZ * WY, 8, 2 * C), 1) < SX
+    return [
+        pltpu.roll(jnp.where(early, right, left), SX, 1).reshape(WT, 2 * C)
+        for left, right in ((first, second), (second, border))
+    ]
+
+
+def columns_of(windows):
+    early = iota((WZ * WY, 8, C), 1) < SX
+    first, second = (pltpu.roll(w.reshape(WZ * WY, 8, C), SX, 1) for w in windows)
+    block = jnp.concatenate([first, jnp.where(early, first, second)], 1)
+    return block.reshape(WZ, WY, 16, C), second.reshape(WZ, WY, 8, C)
 
 
 def kernel(
     scale,
     flags_ref,
-    own_ref,
-    y_ref,
     z_ref,
     zy_ref,
-    gain_ref,
-    beta_ref,
+    y_ref,
+    own_ref,
+    border_ref,
+    norm_ref,
     w_ref,
     wt_ref,
     qkv_bias_ref,
     qkv_bias_t_ref,
     proj_ref,
     table_ref,
-    own_grad_ref,
-    y_grad_ref,
-    z_grad_ref,
-    zy_grad_ref,
+    grad_ref,
+    border_grad_ref,
     sums_ref,
     xhat_s,
     rstd_s,
@@ -156,16 +173,18 @@
     pen_s,
     table_s,
 ):
-    gain = gain_ref[...]
-    beta = beta_ref[...]
+    gain = norm_ref[0:1, :]
+    beta = norm_ref[1:2, :]
     lane = iota((8, WT), 1)
     lane_row = iota((1, WT), 1)
     sub_col = iota((WT, 1), 0)
 
+    block = block_of(own_ref, y_ref, z_ref, zy_ref)
+    border = jnp.concatenate([border_ref[SZ:], border_ref[:SZ]], 0).astype(F32)
+    both = windows_of(block, border.reshape(WZ * WY, SX, 2 * C))
     for w in range(2):
-        parts = (own_ref, y_ref, z_ref, zy_ref)
-        tok = quadrants(*(ref.at[0] for ref in parts), 8 * w)
-        cot = quadrants(*(ref.at[1] for ref in parts), 8 * w).astype(BF16)
+        tok = both[w][:, :C]
+        cot = both[w][:, C:].astype(BF16)
         mean = jnp.mean(tok, -1, keepdims=True)
         centred = tok - mean
         rstd = lax.rsqrt(jnp.mean(centred * centred, -1, keepdims=True) + EPSILON)
@@ -217,6 +236,7 @@
 
     totals = [None] * 4
     vectors = [None] * 5
+    grads = []
 
     def add(store, at, term):
         store[at] = term if store[at] is None else store[at] + term
@@ -240,13 +260,11 @@
         first = jnp.mean(d_xhat, -1, keepdims=True)
         second = jnp.mean(d_xhat * xhat, -1, keepdims=True)
         grad = cot.astype(F32) + rstd_s[w] * (d_xhat - first - xhat * second)
-        grad = grad.reshape(WZ, WY, 8, C).astype(BF16)
-        cols = slice(8 * w, 8 * w + 8)
-        own_grad_ref[:, :, cols, :] = grad[:SZ, :SY]
-        y_grad_ref[:, :, cols, :] = grad[:SZ, SY:]
-        z_grad_ref[:, :, cols, :] = grad[SZ:, :SY]
-        zy_grad_ref[:, :, cols, :] = grad[SZ:, SY:]
-
+        grads.append(grad)
+
+    block, border = columns_of(grads)
+    grad_ref[...] = block.astype(BF16)
+    border_grad_ref[...] = border.astype(BF16)
     for p in range(4):
         sums_ref[C * p : C * p + C, :] = totals[p][:, :128] * scale
     for p in range(2):
@@ -258,11 +276,12 @@
             table_s[c, 6:7, :C] = vectors[c]
         sums_ref[TABLE_ROWS + 16 * c : TABLE_ROWS + 16 * c + 8, :] = table_s[c, :, :128] * scale
         sums_ref[TABLE_ROWS + 16 * c + 8 : TABLE_ROWS + 16 * c + 16, :] = table_s[c, :, 128:] * scale
-
-
-def finish_kernel(sums_ref, qkv_ref, proj_ref, vectors_ref, table_ref):
-    firsts = [sums_ref[C * p : C * p + C, :] for p in range(4)]
-    rests = [sums_ref[C * (4 + p) : C * (5 + p), :] for p in range(2)]
+    sums_ref[USED:, :] = jnp.zeros((ROWS - USED, 128), F32)
+
+
+def finish_kernel(sums_ref, gain_ref, shift_ref, qkv_ref, bias_ref, proj_ref, table_ref):
+    firsts = [sums_ref[C * p : C * p + C, :].astype(F32) for p in range(4)]
+    rests = [sums_ref[C * (4 + p) : C * (5 + p), :].astype(F32) for p in range(2)]
     parts = []
     for p in range(4):
         rest = rests[p // 2]
@@ -272,9 +291,12 @@
     classes = []
     for c in range(8):
         at = TABLE_ROWS + 16 * c
-        classes.append(jnp.concatenate([sums_ref[at : at + 8, :], sums_ref[at + 8 : at + 16, :]], 1))
-    for c in range(5):
-        vectors_ref[c : c + 1, :] = classes[c][6:7, :C]
+        pair = sums_ref[at : at + 16, :].astype(F32)
+        classes.append(jnp.concatenate([pair[:8], pair[8:]], 1))
+    vectors = [classes[c][6:7, :C] for c in range(5)]
+    bias_ref[...] = jnp.concatenate(vectors[:3], 1)[0]
+    gain_ref[...] = vectors[3][0]
+    shift_ref[...] = vectors[4][0]
     block = iota((8, WT), 1) // 64
     rows = []
     for index in range(1, 2 * WZ):
@@ -305,14 +327,12 @@
     vmem = pl.BlockSpec(memory_space=pltpu.VMEM)
     return pl.pallas_call(
         finish_kernel,
-        out_shape=(
-            jax.ShapeDtypeStruct((C, 3 * C), F32),
-            jax.ShapeDtypeStruct((C, C), F32),
-            jax.ShapeDtypeStruct((5, C), F32),
-            jax.ShapeDtypeStruct((HEADS, TABLE), F32),
+        out_shape=tuple(
+            jax.ShapeDtypeStruct(shape, F32)
+            for shape in ((C,), (C,), (C, 3 * C), (3 * C,), (C, C), (HEADS, TABLE))
         ),
         in_specs=[vmem],
-        out_specs=(vmem,) * 4,
+        out_specs=(vmem,) * 6,
         compiler_params=pltpu.CompilerParams(vmem_limit_bytes=16 * 1024 * 1024),
         name="finish",
     )(sums)
@@ -320,12 +340,15 @@
 
 def windows(scale, *operands):
     vmem = pl.BlockSpec(memory_space=pltpu.VMEM)
-    quarter = jax.ShapeDtypeStruct((SZ, SY, 16, C), BF16)
     return pl.pallas_call(
         functools.partial(kernel, scale),
-        out_shape=(quarter,) * 4 + (jax.ShapeDtypeStruct((ROWS, 128), F32),),
+        out_shape=(
+            jax.ShapeDtypeStruct((WZ, WY, 16, C), BF16),
+            jax.ShapeDtypeStruct((WZ, WY, 8, C), BF16),
+            jax.ShapeDtypeStruct((ROWS, 128), F32),
+        ),
         in_specs=[pl.BlockSpec(memory_space=pltpu.SMEM)] + [vmem] * (len(operands) - 1),
-        out_specs=(vmem,) * 5,
+        out_specs=(vmem,) * 3,
         scratch_shapes=[
             pltpu.VMEM((2, WT, C), F32),
             pltpu.VMEM((2, WT, 1), F32),
@@ -363,24 +386,20 @@
     return lax.ppermute(value, tuple(axes), pairs)
 
 
-def shift_pair(stacked):
-    border = sent(stacked[:, :, :, :SX], gx=-1)
-    stacked = jnp.concatenate([stacked[:, :, :, SX:], border], 3)
-    y_part = sent(stacked[:, SZ:, :SY], gy=-1)
-    z_part = sent(stacked[:, :SZ, SY:], gz=-1)
-    zy_part = sent(stacked[:, :SZ, :SY], gz=-1, gy=-1)
-    return stacked[:, SZ:, SY:], y_part, z_part, zy_part
-
-
-def unshift_quarters(own, y_part, z_part, zy_part):
-    y_part = sent(y_part, gy=1)
-    z_part = sent(z_part, gz=1)
-    zy_part = sent(zy_part, gz=1, gy=1)
-    near = jnp.concatenate([zy_part, z_part], 1)
-    far = jnp.concatenate([y_part, own], 1)
-    field = jnp.concatenate([near, far], 0)
-    border = sent(field[:, :, -SX:], gx=1)
-    return jnp.concatenate([border, field[:, :, :-SX]], 2)
+def shift_pair(tokens, grad_out):
+    z_part = jnp.concatenate([tokens[:SZ, SY:], grad_out[:SZ, SY:]], -1)
+    z_part, rest = after(z_part, (tokens, grad_out))
+    both = jnp.concatenate(rest, -1)
+    z_part = sent(z_part, gz=-1)
+    zy_part = sent(both[:SZ, :SY], gz=-1, gy=-1)
+    y_part = sent(both[SZ:, :SY], gy=-1)
+    own = both[SZ:, SY:]
+    far, near = (
+        jnp.concatenate([v[:, :, :SX] for v in pair], 1)
+        for pair in ((z_part, zy_part), (own, y_part))
+    )
+    border = sent(jnp.concatenate([far, near], 0), gx=-1)
+    return z_part, zy_part, y_part, own, border
 
 
 def classes_of(bias_table):
@@ -394,42 +413,51 @@
     return lax.ppermute(value, axis, list(enumerate(partners)))
 
 
-def to_each(value, axis):
-    count = lax.axis_size(axis)
+def to_each(value, axes):
+    count = lax.axis_size(axes)
     spread = jnp.broadcast_to(value[None], (count,) + value.shape)
-    return lax.all_to_all(spread, axis, 0, 0, tiled=True)
-
-
-def reduce_sums(sums):
+    return lax.all_to_all(spread, axes, 0, 0, tiled=True)
+
+
+def after(value, other):
+    return lax.optimization_barrier((value, other))
+
+
+def unshift_and_reduce(field, border, sums):
     half = ROWS // 2
     core = lax.axis_index("gx")
     mine = lax.dynamic_slice_in_dim(sums, core * half, half, 0)
     other = lax.dynamic_slice_in_dim(sums, (1 - core) * half, half, 0)
     mine = mine + swapped(other, "gx", (1, 0))
-    count = lax.axis_size("gy")
-    part = lax.all_to_all(mine.reshape(count, half // count, 128), "gy", 0, 0, tiled=True).sum(0)
-    part = part + swapped(part, "yh", (1, 0, 3, 2))
-    part = part + swapped(part, "yh", (3, 2, 1, 0))
-    part = to_each(part, "z").sum(0)
-    mine = to_each(part, "gy").reshape(half, 128)
-    return lax.all_gather(mine, "gx", axis=0, tiled=True)
+    border = sent(border, gx=1)[:, :, :SX]
+    field = jnp.concatenate([border, field[:, :, SX:]], 2)
+    y_border = sent(field[:, SY:], gy=1)
+    count = lax.axis_size(PLANE)
+    part = lax.all_to_all(mine.reshape(count, half // count, 128), PLANE, 0, 0, tiled=True).sum(0)
+    part, y_border = after(part, y_border)
+    field = jnp.concatenate([y_border, field[:, :SY]], 1)
+    z_border = sent(field[SZ:], gz=1)
+    part = to_each(part, "z").sum(0).astype(BF16)
+    mine = to_each(part, PLANE).reshape(half, 128)
+    outputs = finish(lax.all_gather(mine, "gx", axis=0, tiled=True))
+    outputs, z_border = after(outputs, z_border)
+    return jnp.concatenate([z_border, field[:SZ]], 0), *outputs
 
 
 def per_device(tokens, ln_gain, ln_bias, qkv_weight, qkv_bias, proj_weight, bias_table, grad_out):
     count = tokens.shape[0] * tokens.shape[1] * tokens.shape[2]
     for axis in AXES:
         count *= lax.axis_size(axis)
-    quarters = shift_pair(jnp.stack([tokens, grad_out], 0))
+    quarters = shift_pair(tokens, grad_out)
     w3 = qkv_weight.reshape(C, 3, C).transpose(1, 0, 2)
     w3t = qkv_weight.T.reshape(3, C, C)
     last = [lax.axis_index(a) == lax.axis_size(a) - 1 for a in AXES]
     flags = jnp.stack([last[0] & last[1], last[2], last[3]]).astype(jnp.int32)
-    *grads, sums = windows(
+    field, border, sums = windows(
         1.0 / math.sqrt(count),
         flags,
         *quarters,
-        ln_gain.reshape(1, C),
-        ln_bias.reshape(1, C),
+        jnp.stack([ln_gain, ln_bias], 0),
         w3,
         w3t,
         qkv_bias.reshape(3, 1, C),
@@ -437,17 +465,7 @@
         proj_weight,
         classes_of(bias_table),
     )
-    grad_tokens = unshift_quarters(*grads)
-    grad_qkv, grad_proj, vectors, grad_table = finish(reduce_sums(sums))
-    return (
-        grad_tokens,
-        vectors[3],
-        vectors[4],
-        grad_qkv,
-        vectors[:3].reshape(3 * C),
-        grad_proj,
-        grad_table,
-    )
+    return unshift_and_reduce(field, border, sums)
 
 
 def solution(mesh):

time: 124 us -> 106 us (0.85)
  blocking collectives: 31.2 us -> 17.3 us
  starting transfers between devices: 53.1 us -> 49.4 us
    all_to_all x2 -> x1, blocking collectives: 28.9 us -> 11.6 us  [to_each(): return lax.all_to_all(spread, axes, 0, 0, tiled=True)]
    all_to_all x1 -> x2, waiting for transfers between devices: 0.01 us -> 14.3 us  [the longest x1 7.47 us: to_each(): return lax.all_to_all(spread, axes, 0, 0, tiled=True)]
    all_to_all x1 -> x2, starting transfers between devices: 3.43 us -> 13.3 us  [the longest x1 6.93 us: unshift_and_reduce(): lax.all_to_all(mine.reshape(count, half // count, 128), PLANE, 0, 0, tile...]
    ppermute x8 -> x7, waiting for transfers between devices: 10.9 us -> 2.72 us  [sent(): return lax.ppermute(value, tuple(axes), pairs)]
    ppermute x3 -> x1, waiting for transfers between devices: 8.36 us -> 1.33 us  [swapped(): return lax.ppermute(value, axis, list(enumerate(partners)))]
    ppermute x3 -> x1, starting transfers between devices: 9.12 us -> 2.27 us  [swapped(): return lax.ppermute(value, axis, list(enumerate(partners)))]
    ppermute x8 -> x7, starting transfers between devices: 40.5 us -> 33.8 us  [sent(): return lax.ppermute(value, tuple(axes), pairs)]
    all_gather x1, blocking collectives: 2.26 us -> 5.72 us  [unshift_and_reduce(): outputs = finish(lax.all_gather(mine, 'gx', axis=0, tiled=True))]
  transfers between devices with their start and end apart: 12 -> 10, of which waited for: 9 -> 6; matrix products, arithmetic and copies ran while one was open for 3% -> 2% of each run, Pallas kernels for 0% -> 1%
where the time goes in v2:
time: 106 us; the launch traced here: 105 us
  starting transfers between devices  49.4 us (47%)
  waiting for transfers between devices  18.4 us (17%)
  blocking collectives  17.3 us (16%)
  Pallas kernels  9.23 us (9%)
  local copies, waits for them, and re-layouts  6.46 us (6%)
  other arithmetic  3.03 us (3%)
    ppermute x7, starting transfers between devices, sent(): return lax.ppermute(value, tuple(axes), pairs)  33.8 us
    all_to_all x1, blocking collectives, to_each(): return lax.all_to_all(spread, axes, 0, 0, tiled=True)  11.6 us
    pallas_call x1, Pallas kernels, windows(): pl.pallas_call(functools.partial(kernel, scale), out_shape=(jax.ShapeDtyp...  8 us
    all_to_all x1, waiting for transfers between devices, to_each(): return lax.all_to_all(spread, axes, 0, 0, tiled=True)  7.47 us
    all_to_all x1, starting transfers between devices, unshift_and_reduce(): lax.all_to_all(mine.reshape(count, half // count, 128), PLANE, 0, 0, tile...  6.93 us
    all_to_all x1, waiting for transfers between devices, unshift_and_reduce(): lax.all_to_all(mine.reshape(count, half // count, 128), PLANE, 0, 0, tile...  6.85 us
    all_to_all x1, starting transfers between devices, to_each(): return lax.all_to_all(spread, axes, 0, 0, tiled=True)  6.35 us
    all_gather x1, blocking collectives, unshift_and_reduce(): outputs = finish(lax.all_gather(mine, 'gx', axis=0, tiled=True))  5.72 us
  transfers between devices with their start and end apart: 10, of which 6 were waited for; matrix products, arithmetic and copies ran while one was open for 2% of the time, Pallas kernels for 1%

profile of v2, /device:TPU:1, one launch (start us, length us, event | category | flops | bytes accessed | tf_op | source)
XLA Modules:
  0.0 104.8 jit_solution(2144539525944690444)
XLA Ops:
  0.6 0.9 slice.46
  1.5 0.8 slice.47
  2.5 1.0 fusion.10
  3.5 16.6 %collective-permute-start.1 = (bf16[2,4,16,384]{3,2,1,0:T(8,128)(2,1)S(1)}, bf16[2,4,16,384]{3,2,1,0:T(8,128)(2,1)S(1)}, u32[]{:S(2)}, u32[]{:S(2)}) collective-permute-start(bf16[2,4,16,384]{3,2,1,0:T(8,128)(2,1)S(1)} %get-tuple-element.50), channel_id=1, source_target_pairs={{0,510},{2,496},{4,498},{6,500},{8,502},{10,504},{12,506},{14,508}... | collective-permute-start | bytes 294920 | tf_op jit(solution)/shard_map/ppermute | solution.py:386
  20.1 3.4 %collective-permute-start.2 = (bf16[2,4,16,384]{3,2,1,0:T(8,128)(2,1)S(1)}, bf16[2,4,16,384]{3,2,1,0:T(8,128)(2,1)S(1)}, u32[]{:S(2)}, u32[]{:S(2)}) collective-permute-start(bf16[2,4,16,384]{3,2,1,0:T(8,128)(2,1)S(1)} %get-tuple-element.51), channel_id=1, source_target_pairs={{0,14},{2,0},{4,2},{6,4},{8,6},{10,8},{12,10},{14,12},{1,15},{3,1}... | collective-permute-start | bytes 294920 | tf_op jit(solution)/shard_map/ppermute | solution.py:386
  23.5 2.2 %collective-permute-start = (bf16[2,4,16,384]{3,2,1,0:T(8,128)(2,1)S(1)}, bf16[2,4,16,384]{3,2,1,0:T(8,128)(2,1)S(1)}, u32[]{:S(2)}, u32[]{:S(2)}) collective-permute-start(bf16[2,4,16,384]{3,2,1,0:T(8,128)(2,1)S(1)} %pad_maximum_fusion.2), channel_id=1, source_target_pairs={{0,496},{16,0},{32,16},{48,32},{64,48},{80,64},{96,80},{112,96},{1... | collective-permute-start | bytes 294920 | tf_op jit(solution)/shard_map/ppermute | solution.py:386
  25.7 0.2 reshape.54.qkv_bias_t_ref
  26.0 0.5 copy-done.4
  26.9 0.5 reshape.50
  27.5 0.4 reshape.51.table_ref
  27.9 0.5 copy-done.3
  29.0 0.5 copy-done.7
  29.8 3.4 %collective-permute-start.3 = (bf16[4,8,4,384]{3,2,1,0:T(4,128)(2,1)S(1)}, bf16[4,8,4,384]{3,2,1,0:T(4,128)(2,1)S(1)}, u32[]{:S(2)}, u32[]{:S(2)}) collective-permute-start(bf16[4,8,4,384]{3,2,1,0:T(4,128)(2,1)S(1)} %fusion.8), channel_id=1, source_target_pairs={{0,1},{1,0},{2,3},{3,2},{4,5},{5,4},{6,7},{7,6},{8,9},{9,8},{10,11... | collective-permute-start | bytes 294920 | tf_op jit(solution)/shard_map/ppermute | solution.py:386
  33.4 0.8 collective-permute-done.3.border_ref
  34.2 8.0 %windows.1 = (bf16[4,8,16,192]{3,2,1,0:T(8,128)(2,1)S(1)}, bf16[4,8,8,192]{3,2,1,0:T(8,128)(2,1)S(1)}, f32[1536,128]{1,0:T(8,128)S(1)}) custom-call(s32[3]{0:T(128)S(1)} %add_convert_fusion.flags_ref, bf16[2,4,16,384]{3,2,1,0:T(8,128)(2,1)S(1)} %collective-permute-done.z_ref, bf16[2,4,16,384]{3,2,1,0:T(8,128)(2,1)S(1)} %collective-permute-done.1.zy_ref, ...), custom_call_target="tpu_custom_call" | custom-call | flops 1000000000 | bytes 3000000 | tf_op jit(solution)/shard_map/windows/pallas_call | solution.py:343
  42.3 2.3 %collective-permute-start.4 = (f32[768,128]{1,0:T(8,128)S(1)}, f32[768,128]{1,0:T(8,128)S(1)}, u32[]{:S(2)}, u32[]{:S(2)}) collective-permute-start(f32[768,128]{1,0:T(8,128)S(1)} %constant_dynamic-slice_fusion), channel_id=1, source_target_pairs={{0,1},{1,0},{2,3},{3,2},{4,5},{5,4},{6,7},{7,6},{8,9},{9,8},{10,11... | collective-permute-start | bytes 1179656 | tf_op jit(solution)/shard_map/ppermute | solution.py:413
  44.6 1.3 %collective-permute-done.4 = f32[768,128]{1,0:T(8,128)S(1)} collective-permute-done((f32[768,128]{1,0:T(8,128)S(1)}, f32[768,128]{1,0:T(8,128)S(1)}, u32[]{:S(2)}, u32[]{:S(2)}) %collective-permute-start.4) | collective-permute-done | bytes 393248 | tf_op jit(solution)/shard_map/ppermute | solution.py:413
  45.9 0.8 dynamic-slice_add_fusion
  46.7 6.9 %all-to-all-start = ((f32[32,24,128]{2,1,0:T(8,128)}), f32[32,24,128]{2,1,0:T(8,128)S(1)}, u32[]{:S(2)}, u32[]{:S(2)}) async-start(f32[32,24,128]{2,1,0:T(8,128)} %bitcast.10), calls=%async_computation | async-start | bytes 786432 | tf_op jit(solution)/shard_map/all_to_all | solution.py:436
  53.6 2.5 %collective-permute-start.5 = (bf16[4,8,8,192]{3,2,1,0:T(8,128)(2,1)S(1)}, bf16[4,8,8,192]{3,2,1,0:T(8,128)(2,1)S(1)}, u32[]{:S(2)}, u32[]{:S(2)}) collective-permute-start(bf16[4,8,8,192]{3,2,1,0:T(8,128)(2,1)S(1)} %get-tuple-element.32), channel_id=1, source_target_pairs={{0,1},{1,0},{2,3},{3,2},{4,5},{5,4},{6,7},{7,6},{8,9},{9,8},{10,11... | collective-permute-start | bytes 294920 | tf_op jit(solution)/shard_map/ppermute | solution.py:386
  56.2 0.9 collective-permute-done.5
  57.2 3.4 %collective-permute-start.6 = (bf16[4,4,16,192]{3,2,1,0:T(8,128)(2,1)S(1)}, bf16[4,4,16,192]{3,2,1,0:T(8,128)(2,1)S(1)}, u32[]{:S(2)}, u32[]{:S(2)}) collective-permute-start(bf16[4,4,16,192]{3,2,1,0:T(8,128)(2,1)S(1)} %fusion.4), channel_id=1, source_target_pairs={{0,2},{2,4},{4,6},{6,8},{8,10},{10,12},{12,14},{14,0},{1,3},{3,5},... | collective-permute-start | bytes 294920 | tf_op jit(solution)/shard_map/ppermute | solution.py:386
  60.6 6.9 %all-to-all-done = f32[32,24,128]{2,1,0:T(8,128)S(1)} async-done(((f32[32,24,128]{2,1,0:T(8,128)}), f32[32,24,128]{2,1,0:T(8,128)S(1)}, u32[]{:S(2)}, u32[]{:S(2)}) %all-to-all-start) | async-done | bytes 393248 | tf_op jit(solution)/shard_map/all_to_all | solution.py:436
  67.5 1.0 collective-permute-done.6
  68.5 11.6 %all_to_all.15 = f32[8,24,128]{2,1,0:T(8,128)S(1)} all-to-all(f32[8,24,128]{2,1,0:T(8,128)S(1)} %broadcast_in_dim.4), channel_id=1, replica_groups=mesh['yh'=4,'z'=8,'gy'=8,'gx'=2] {'z'}, dimensions={0} | all-to-all | bytes 196608 | tf_op jit(solution)/shard_map/all_to_all | solution.py:419
  80.2 0.7 broadcast_in_dim.5
  80.9 6.3 %all-to-all-start.2 = ((bf16[32,24,128]{2,1,0:T(8,128)(2,1)}), bf16[32,24,128]{2,1,0:T(8,128)(2,1)S(1)}, u32[]{:S(2)}, u32[]{:S(2)}) async-start(bf16[32,24,128]{2,1,0:T(8,128)(2,1)} %broadcast_in_dim.5), calls=%async_computation.2 | async-start | bytes 393216 | tf_op jit(solution)/shard_map/all_to_all | solution.py:419
  87.3 2.3 %collective-permute-start.7 = (bf16[2,8,16,192]{3,2,1,0:T(8,128)(2,1)S(1)}, bf16[2,8,16,192]{3,2,1,0:T(8,128)(2,1)S(1)}, u32[]{:S(2)}, u32[]{:S(2)}) collective-permute-start(bf16[2,8,16,192]{3,2,1,0:T(8,128)(2,1)S(1)} %get-tuple-element.52), channel_id=1, source_target_pairs={{0,16},{16,32},{32,48},{48,64},{64,80},{80,96},{96,112},{112,128},... | collective-permute-start | bytes 294920 | tf_op jit(solution)/shard_map/ppermute | solution.py:386
  89.6 7.5 %all-to-all-done.2 = bf16[32,24,128]{2,1,0:T(8,128)(2,1)S(1)} async-done(((bf16[32,24,128]{2,1,0:T(8,128)(2,1)}), bf16[32,24,128]{2,1,0:T(8,128)(2,1)S(1)}, u32[]{:S(2)}, u32[]{:S(2)}) %all-to-all-start.2) | async-done | bytes 196640 | tf_op jit(solution)/shard_map/all_to_all | solution.py:419
  97.1 5.7 %all_gather.3.sums_ref = bf16[1536,128]{1,0:T(8,128)(2,1)S(1)} all-gather(bf16[768,128]{1,0:T(8,128)(2,1)S(1)} %bitcast.21), channel_id=1, replica_groups=mesh['yh'=4,'z'=8,'gy'=8,'gx'=2] {'gx'}, dimensions={0}, use_global_device_ids=true | all-gather | bytes 589824 | tf_op jit(solution)/shard_map/all_gather | solution.py:442
  102.8 1.2 %finish.1 = (f32[192]{0:T(256)}, f32[192]{0:T(256)}, f32[192,576]{1,0:T(8,128)}, f32[576]{0:T(1024)}, f32[192,192]{1,0:T(8,128)}, /*index=5*/f32[6,1575]{1,0:T(8,128)}) custom-call(bf16[1536,128]{1,0:T(8,128)(2,1)S(1)} %all_gather.3.sums_ref), custom_call_target="tpu_custom_call" | custom-call | tf_op jit(solution)/shard_map/finish/pallas_call | solution.py:328
  104.1 0.7 pad_maximum_fusion.1
  (40 shorter events, 1.9 us)
Async XLA Ops:
  0.6 1.8 %copy-start.1 = (bf16[4,8,16,192]{3,2,1,0:T(8,128)(2,1)S(1)}, bf16[4,8,16,192]{3,2,1,0:T(8,128)(2,1)}, u32[]{:S(2)}) copy-start(bf16[4,8,16,192]{3,2,1,0:T(8,128)(2,1)} %param.15) | copy-start | bytes 589828
  3.5 22.2 %copy-start.5 = (f32[576]{0:T(1024)S(1)}, f32[576]{0:T(1024)}, u32[]{:S(2)}) copy-start(f32[576]{0:T(1024)} %param.12) | copy-start | bytes 6916
  3.5 26.1 %collective-permute-start.1 = (bf16[2,4,16,384]{3,2,1,0:T(8,128)(2,1)S(1)}, bf16[2,4,16,384]{3,2,1,0:T(8,128)(2,1)S(1)}, u32[]{:S(2)}, u32[]{:S(2)}) collective-permute-start(bf16[2,4,16,384]{3,2,1,0:T(8,128)(2,1)S(1)} %get-tuple-element.50), channel_id=1, source_target_pairs={{0,510},{2,496},{4,498},{6,500},{8,502},{10,504},{12,506},{14,508}... | collective-permute-start | bytes 294920 | tf_op jit(solution)/shard_map/ppermute | solution.py:386
  20.1 9.5 %collective-permute-start.2 = (bf16[2,4,16,384]{3,2,1,0:T(8,128)(2,1)S(1)}, bf16[2,4,16,384]{3,2,1,0:T(8,128)(2,1)S(1)}, u32[]{:S(2)}, u32[]{:S(2)}) collective-permute-start(bf16[2,4,16,384]{3,2,1,0:T(8,128)(2,1)S(1)} %get-tuple-element.51), channel_id=1, source_target_pairs={{0,14},{2,0},{4,2},{6,4},{8,6},{10,8},{12,10},{14,12},{1,15},{3,1}... | collective-permute-start | bytes 294920 | tf_op jit(solution)/shard_map/ppermute | solution.py:386
  23.5 6.2 %collective-permute-start = (bf16[2,4,16,384]{3,2,1,0:T(8,128)(2,1)S(1)}, bf16[2,4,16,384]{3,2,1,0:T(8,128)(2,1)S(1)}, u32[]{:S(2)}, u32[]{:S(2)}) collective-permute-start(bf16[2,4,16,384]{3,2,1,0:T(8,128)(2,1)S(1)} %pad_maximum_fusion.2), channel_id=1, source_target_pairs={{0,496},{16,0},{32,16},{48,32},{64,48},{80,64},{96,80},{112,96},{1... | collective-permute-start | bytes 294920 | tf_op jit(solution)/shard_map/ppermute | solution.py:386
  25.7 0.8 copy-start.4
  27.5 1.0 copy-start.3
  28.7 0.7 copy-start.7
  28.8 1.0 copy-start.2
  29.0 0.7 copy-start.6
  29.7 4.5 %copy-start = (bf16[192,192]{1,0:T(8,128)(2,1)S(1)}, bf16[192,192]{1,0:T(8,128)(2,1)}, u32[]{:S(2)}) copy-start(bf16[192,192]{1,0:T(8,128)(2,1)} %proj_ref.1) | copy-start | bytes 221188
  29.8 4.4 %collective-permute-start.3 = (bf16[4,8,4,384]{3,2,1,0:T(4,128)(2,1)S(1)}, bf16[4,8,4,384]{3,2,1,0:T(4,128)(2,1)S(1)}, u32[]{:S(2)}, u32[]{:S(2)}) collective-permute-start(bf16[4,8,4,384]{3,2,1,0:T(4,128)(2,1)S(1)} %fusion.8), channel_id=1, source_target_pairs={{0,1},{1,0},{2,3},{3,2},{4,5},{5,4},{6,7},{7,6},{8,9},{9,8},{10,11... | collective-permute-start | bytes 294920 | tf_op jit(solution)/shard_map/ppermute | solution.py:386
  42.3 3.6 %collective-permute-start.4 = (f32[768,128]{1,0:T(8,128)S(1)}, f32[768,128]{1,0:T(8,128)S(1)}, u32[]{:S(2)}, u32[]{:S(2)}) collective-permute-start(f32[768,128]{1,0:T(8,128)S(1)} %constant_dynamic-slice_fusion), channel_id=1, source_target_pairs={{0,1},{1,0},{2,3},{3,2},{4,5},{5,4},{6,7},{7,6},{8,9},{9,8},{10,11... | collective-permute-start | bytes 1179656 | tf_op jit(solution)/shard_map/ppermute | solution.py:413
  46.7 20.8 %all-to-all-start = ((f32[32,24,128]{2,1,0:T(8,128)}), f32[32,24,128]{2,1,0:T(8,128)S(1)}, u32[]{:S(2)}, u32[]{:S(2)}) async-start(f32[32,24,128]{2,1,0:T(8,128)} %bitcast.10), calls=%async_computation | async-start | bytes 786432 | tf_op jit(solution)/shard_map/all_to_all | solution.py:436
  53.6 3.5 %collective-permute-start.5 = (bf16[4,8,8,192]{3,2,1,0:T(8,128)(2,1)S(1)}, bf16[4,8,8,192]{3,2,1,0:T(8,128)(2,1)S(1)}, u32[]{:S(2)}, u32[]{:S(2)}) collective-permute-start(bf16[4,8,8,192]{3,2,1,0:T(8,128)(2,1)S(1)} %get-tuple-element.32), channel_id=1, source_target_pairs={{0,1},{1,0},{2,3},{3,2},{4,5},{5,4},{6,7},{7,6},{8,9},{9,8},{10,11... | collective-permute-start | bytes 294920 | tf_op jit(solution)/shard_map/ppermute | solution.py:386
  57.2 11.3 %collective-permute-start.6 = (bf16[4,4,16,192]{3,2,1,0:T(8,128)(2,1)S(1)}, bf16[4,4,16,192]{3,2,1,0:T(8,128)(2,1)S(1)}, u32[]{:S(2)}, u32[]{:S(2)}) collective-permute-start(bf16[4,4,16,192]{3,2,1,0:T(8,128)(2,1)S(1)} %fusion.4), channel_id=1, source_target_pairs={{0,2},{2,4},{4,6},{6,8},{8,10},{10,12},{12,14},{14,0},{1,3},{3,5},... | collective-permute-start | bytes 294920 | tf_op jit(solution)/shard_map/ppermute | solution.py:386
  80.9 16.2 %all-to-all-start.2 = ((bf16[32,24,128]{2,1,0:T(8,128)(2,1)}), bf16[32,24,128]{2,1,0:T(8,128)(2,1)S(1)}, u32[]{:S(2)}, u32[]{:S(2)}) async-start(bf16[32,24,128]{2,1,0:T(8,128)(2,1)} %broadcast_in_dim.5), calls=%async_computation.2 | async-start | bytes 393216 | tf_op jit(solution)/shard_map/all_to_all | solution.py:419
  87.3 16.7 %collective-permute-start.7 = (bf16[2,8,16,192]{3,2,1,0:T(8,128)(2,1)S(1)}, bf16[2,8,16,192]{3,2,1,0:T(8,128)(2,1)S(1)}, u32[]{:S(2)}, u32[]{:S(2)}) collective-permute-start(bf16[2,8,16,192]{3,2,1,0:T(8,128)(2,1)S(1)} %get-tuple-element.52), channel_id=1, source_target_pairs={{0,16},{16,32},{32,48},{48,64},{64,80},{80,96},{96,112},{112,128},... | collective-permute-start | bytes 294920 | tf_op jit(solution)/shard_map/ppermute | solution.py:386

commit v3 on v2

--- a/solution.py
+++ b/solution.py
@@ -387,10 +387,8 @@
 
 
 def shift_pair(tokens, grad_out):
-    z_part = jnp.concatenate([tokens[:SZ, SY:], grad_out[:SZ, SY:]], -1)
-    z_part, rest = after(z_part, (tokens, grad_out))
-    both = jnp.concatenate(rest, -1)
-    z_part = sent(z_part, gz=-1)
+    both = jnp.concatenate([tokens, grad_out], -1)
+    z_part = sent(both[:SZ, SY:], gz=-1)
     zy_part = sent(both[:SZ, :SY], gz=-1, gy=-1)
     y_part = sent(both[SZ:, :SY], gy=-1)
     own = both[SZ:, SY:]
@@ -434,10 +432,11 @@
     y_border = sent(field[:, SY:], gy=1)
     count = lax.axis_size(PLANE)
     part = lax.all_to_all(mine.reshape(count, half // count, 128), PLANE, 0, 0, tiled=True).sum(0)
+    part, field = after(part, field)
+    part = to_each(part, "z").sum(0).astype(BF16)
     part, y_border = after(part, y_border)
     field = jnp.concatenate([y_border, field[:, :SY]], 1)
     z_border = sent(field[SZ:], gz=1)
-    part = to_each(part, "z").sum(0).astype(BF16)
     mine = to_each(part, PLANE).reshape(half, 128)
     outputs = finish(lax.all_gather(mine, "gx", axis=0, tiled=True))
     outputs, z_border = after(outputs, z_border)

time: 106 us -> 103 us (0.972)
  blocking collectives: 17.3 us -> 6.04 us
  waiting for transfers between devices: 18.4 us -> 24.9 us
  starting transfers between devices: 49.4 us -> 52 us
  local copies, waits for them, and re-layouts: 6.46 us -> 5.39 us
    all_to_all x1 -> x0, blocking collectives: 11.6 us -> none  [to_each(): return lax.all_to_all(spread, axes, 0, 0, tiled=True)]
    all_to_all x1 -> x2, waiting for transfers between devices: 7.47 us -> 11.3 us  [to_each(): return lax.all_to_all(spread, axes, 0, 0, tiled=True)]
    all_to_all x1, waiting for transfers between devices: 6.85 us -> 10.2 us  [unshift_and_reduce(): lax.all_to_all(mine.reshape(count, half // count, 128), PLANE, 0, 0, tile...]
    all_to_all x1 -> x2, starting transfers between devices: 6.35 us -> 8.24 us  [to_each(): return lax.all_to_all(spread, axes, 0, 0, tiled=True)]
    slice x3 -> x1, local copies, waits for them, and re-layouts: 1.76 us -> 0.01 us  [unshift_and_reduce(): field = jnp.concatenate([y_border, field[:, :SY]], 1)]
  transfers between devices with their start and end apart: 10 -> 11, of which waited for: 6 -> 7; matrix products, arithmetic and copies ran while one was open for 2% -> 2% of each run, Pallas kernels for 1% -> 1%
where the time goes in v3:
time: 103 us; the launch traced here: 102 us
  starting transfers between devices  52 us (50%)
  waiting for transfers between devices  24.9 us (24%)
  Pallas kernels  9.24 us (9%)
  blocking collectives  6.04 us (6%)
  local copies, waits for them, and re-layouts  5.39 us (5%)
  other arithmetic  3.2 us (3%)
    ppermute x7, starting transfers between devices, sent(): return lax.ppermute(value, tuple(axes), pairs)  34.1 us
    all_to_all x2, waiting for transfers between devices, to_each(): return lax.all_to_all(spread, axes, 0, 0, tiled=True)  11.3 us
    all_to_all x1, waiting for transfers between devices, unshift_and_reduce(): lax.all_to_all(mine.reshape(count, half // count, 128), PLANE, 0, 0, tile...  10.2 us
    all_to_all x2, starting transfers between devices, to_each(): return lax.all_to_all(spread, axes, 0, 0, tiled=True)  8.24 us
    pallas_call x1, Pallas kernels, windows(): pl.pallas_call(functools.partial(kernel, scale), out_shape=(jax.ShapeDtyp...  8.01 us
    all_to_all x1, starting transfers between devices, unshift_and_reduce(): lax.all_to_all(mine.reshape(count, half // count, 128), PLANE, 0, 0, tile...  7.35 us
    all_gather x1, blocking collectives, unshift_and_reduce(): outputs = finish(lax.all_gather(mine, 'gx', axis=0, tiled=True))  6.04 us
    ppermute x1, starting transfers between devices, swapped(): return lax.ppermute(value, axis, list(enumerate(partners)))  2.26 us
  transfers between devices with their start and end apart: 11, of which 7 were waited for; matrix products, arithmetic and copies ran while one was open for 2% of the time, Pallas kernels for 1%

profile of v3, /device:TPU:1, one launch (start us, length us, event | category | flops | bytes accessed | tf_op | source)
XLA Modules:
  0.0 101.8 jit_solution(3919709399458553379)
XLA Ops:
  0.6 1.2 %fusion.11 = (bf16[2,4,16,384]{3,2,1,0:T(8,128)(2,1)S(1)}, bf16[2,4,16,384]{3,2,1,0:T(8,128)(2,1)S(1)}, bf16[2,4,16,384]{3,2,1,0:T(8,128)(2,1)S(1)}, bf16[2,4,16,384]{3,2,1,0:T(8,128)(2,1)S(1)}) fusion(bf16[4,8,16,192]{3,2,1,0:T(8,128)(2,1)} %param.8, bf16[4,8,16,192]{3,2,1,0:T(8,128)(2,1)} %param.15), kind=kLoop, calls=%fused_computation.28 | loop fusion | flops 786432 | bytes 786432 | tf_op jit(solution)/shard_map/concatenate | solution.py:390
  1.9 15.2 %collective-permute-start = (bf16[2,4,16,384]{3,2,1,0:T(8,128)(2,1)S(1)}, bf16[2,4,16,384]{3,2,1,0:T(8,128)(2,1)S(1)}, u32[]{:S(2)}, u32[]{:S(2)}) collective-permute-start(bf16[2,4,16,384]{3,2,1,0:T(8,128)(2,1)S(1)} %get-tuple-element.48), channel_id=1, source_target_pairs={{0,496},{16,0},{32,16},{48,32},{64,48},{80,64},{96,80},{112,96},{1... | collective-permute-start | bytes 294920 | tf_op jit(solution)/shard_map/ppermute | solution.py:386
  17.1 3.6 %collective-permute-start.1 = (bf16[2,4,16,384]{3,2,1,0:T(8,128)(2,1)S(1)}, bf16[2,4,16,384]{3,2,1,0:T(8,128)(2,1)S(1)}, u32[]{:S(2)}, u32[]{:S(2)}) collective-permute-start(bf16[2,4,16,384]{3,2,1,0:T(8,128)(2,1)S(1)} %get-tuple-element.49), channel_id=1, source_target_pairs={{0,510},{2,496},{4,498},{6,500},{8,502},{10,504},{12,506},{14,508}... | collective-permute-start | bytes 294920 | tf_op jit(solution)/shard_map/ppermute | solution.py:386
  20.7 3.4 %collective-permute-start.2 = (bf16[2,4,16,384]{3,2,1,0:T(8,128)(2,1)S(1)}, bf16[2,4,16,384]{3,2,1,0:T(8,128)(2,1)S(1)}, u32[]{:S(2)}, u32[]{:S(2)}) collective-permute-start(bf16[2,4,16,384]{3,2,1,0:T(8,128)(2,1)S(1)} %get-tuple-element.50), channel_id=1, source_target_pairs={{0,14},{2,0},{4,2},{6,4},{8,6},{10,8},{12,10},{14,12},{1,15},{3,1}... | collective-permute-start | bytes 294920 | tf_op jit(solution)/shard_map/ppermute | solution.py:386
  24.1 0.2 reshape.52.qkv_bias_t_ref
  24.4 0.5 copy-done.4
  25.2 0.5 reshape.48
  25.8 0.4 reshape.49.table_ref
  26.2 0.5 copy-done.3
  27.3 0.5 copy-done.7
  28.2 3.4 %collective-permute-start.3 = (bf16[4,8,4,384]{3,2,1,0:T(4,128)(2,1)S(1)}, bf16[4,8,4,384]{3,2,1,0:T(4,128)(2,1)S(1)}, u32[]{:S(2)}, u32[]{:S(2)}) collective-permute-start(bf16[4,8,4,384]{3,2,1,0:T(4,128)(2,1)S(1)} %fusion.9), channel_id=1, source_target_pairs={{0,1},{1,0},{2,3},{3,2},{4,5},{5,4},{6,7},{7,6},{8,9},{9,8},{10,11... | collective-permute-start | bytes 294920 | tf_op jit(solution)/shard_map/ppermute | solution.py:386
  31.7 0.8 collective-permute-done.3.border_ref
  32.6 8.0 %windows.1 = (bf16[4,8,16,192]{3,2,1,0:T(8,128)(2,1)S(1)}, bf16[4,8,8,192]{3,2,1,0:T(8,128)(2,1)S(1)}, f32[1536,128]{1,0:T(8,128)S(1)}) custom-call(s32[3]{0:T(128)S(1)} %add_convert_fusion.flags_ref, bf16[2,4,16,384]{3,2,1,0:T(8,128)(2,1)S(1)} %collective-permute-done.z_ref, bf16[2,4,16,384]{3,2,1,0:T(8,128)(2,1)S(1)} %collective-permute-done.1.zy_ref, ...), custom_call_target="tpu_custom_call" | custom-call | flops 1000000000 | bytes 3000000 | tf_op jit(solution)/shard_map/windows/pallas_call | solution.py:343
  40.6 2.3 %collective-permute-start.4 = (f32[768,128]{1,0:T(8,128)S(1)}, f32[768,128]{1,0:T(8,128)S(1)}, u32[]{:S(2)}, u32[]{:S(2)}) collective-permute-start(f32[768,128]{1,0:T(8,128)S(1)} %constant_dynamic-slice_fusion), channel_id=1, source_target_pairs={{0,1},{1,0},{2,3},{3,2},{4,5},{5,4},{6,7},{7,6},{8,9},{9,8},{10,11... | collective-permute-start | bytes 1179656 | tf_op jit(solution)/shard_map/ppermute | solution.py:411
  42.9 1.3 %collective-permute-done.4 = f32[768,128]{1,0:T(8,128)S(1)} collective-permute-done((f32[768,128]{1,0:T(8,128)S(1)}, f32[768,128]{1,0:T(8,128)S(1)}, u32[]{:S(2)}, u32[]{:S(2)}) %collective-permute-start.4) | collective-permute-done | bytes 393248 | tf_op jit(solution)/shard_map/ppermute | solution.py:411
  44.3 0.8 dynamic-slice_add_fusion
  45.0 7.3 %all-to-all-start = ((f32[32,24,128]{2,1,0:T(8,128)}), f32[32,24,128]{2,1,0:T(8,128)S(1)}, u32[]{:S(2)}, u32[]{:S(2)}) async-start(f32[32,24,128]{2,1,0:T(8,128)} %bitcast.10), calls=%async_computation | async-start | bytes 786432 | tf_op jit(solution)/shard_map/all_to_all | solution.py:434
  52.4 2.5 %collective-permute-start.5 = (bf16[4,8,8,192]{3,2,1,0:T(8,128)(2,1)S(1)}, bf16[4,8,8,192]{3,2,1,0:T(8,128)(2,1)S(1)}, u32[]{:S(2)}, u32[]{:S(2)}) collective-permute-start(bf16[4,8,8,192]{3,2,1,0:T(8,128)(2,1)S(1)} %get-tuple-element.28), channel_id=1, source_target_pairs={{0,1},{1,0},{2,3},{3,2},{4,5},{5,4},{6,7},{7,6},{8,9},{9,8},{10,11... | collective-permute-start | bytes 294920 | tf_op jit(solution)/shard_map/ppermute | solution.py:386
  55.0 0.9 collective-permute-done.5
  56.1 10.2 %all-to-all-done = f32[32,24,128]{2,1,0:T(8,128)S(1)} async-done(((f32[32,24,128]{2,1,0:T(8,128)}), f32[32,24,128]{2,1,0:T(8,128)S(1)}, u32[]{:S(2)}, u32[]{:S(2)}) %all-to-all-start) | async-done | bytes 393248 | tf_op jit(solution)/shard_map/all_to_all | solution.py:434
  66.3 0.6 broadcast_in_dim.4
  67.0 3.4 %all-to-all-start.1 = ((f32[8,24,128]{2,1,0:T(8,128)}), f32[8,24,128]{2,1,0:T(8,128)S(1)}, u32[]{:S(2)}, u32[]{:S(2)}) async-start(f32[8,24,128]{2,1,0:T(8,128)} %broadcast_in_dim.4), calls=%async_computation.1 | async-start | bytes 196608 | tf_op jit(solution)/shard_map/all_to_all | solution.py:417
  70.5 2.9 %collective-permute-start.6 = (bf16[4,4,16,192]{3,2,1,0:T(8,128)(2,1)S(1)}, bf16[4,4,16,192]{3,2,1,0:T(8,128)(2,1)S(1)}, u32[]{:S(2)}, u32[]{:S(2)}) collective-permute-start(bf16[4,4,16,192]{3,2,1,0:T(8,128)(2,1)S(1)} %fusion.4), channel_id=1, source_target_pairs={{0,2},{2,4},{4,6},{6,8},{8,10},{10,12},{12,14},{14,0},{1,3},{3,5},... | collective-permute-start | bytes 294920 | tf_op jit(solution)/shard_map/ppermute | solution.py:386
  73.4 4.6 %all-to-all-done.1 = f32[8,24,128]{2,1,0:T(8,128)S(1)} async-done(((f32[8,24,128]{2,1,0:T(8,128)}), f32[8,24,128]{2,1,0:T(8,128)S(1)}, u32[]{:S(2)}, u32[]{:S(2)}) %all-to-all-start.1) | async-done | bytes 98336 | tf_op jit(solution)/shard_map/all_to_all | solution.py:417
  78.0 0.3 collective-permute-done.6
  78.3 0.7 broadcast_in_dim.5
  79.0 4.8 %all-to-all-start.2 = ((bf16[32,24,128]{2,1,0:T(8,128)(2,1)}), bf16[32,24,128]{2,1,0:T(8,128)(2,1)S(1)}, u32[]{:S(2)}, u32[]{:S(2)}) async-start(bf16[32,24,128]{2,1,0:T(8,128)(2,1)} %broadcast_in_dim.5), calls=%async_computation.2 | async-start | bytes 393216 | tf_op jit(solution)/shard_map/all_to_all | solution.py:417
  83.9 3.2 %collective-permute-start.7 = (bf16[2,8,16,192]{3,2,1,0:T(8,128)(2,1)S(1)}, bf16[2,8,16,192]{3,2,1,0:T(8,128)(2,1)S(1)}, u32[]{:S(2)}, u32[]{:S(2)}) collective-permute-start(bf16[2,8,16,192]{3,2,1,0:T(8,128)(2,1)S(1)} %fusion.5), channel_id=1, source_target_pairs={{0,16},{16,32},{32,48},{48,64},{64,80},{80,96},{96,112},{112,128},... | collective-permute-start | bytes 294920 | tf_op jit(solution)/shard_map/ppermute | solution.py:386
  87.0 6.7 %all-to-all-done.2 = bf16[32,24,128]{2,1,0:T(8,128)(2,1)S(1)} async-done(((bf16[32,24,128]{2,1,0:T(8,128)(2,1)}), bf16[32,24,128]{2,1,0:T(8,128)(2,1)S(1)}, u32[]{:S(2)}, u32[]{:S(2)}) %all-to-all-start.2) | async-done | bytes 196640 | tf_op jit(solution)/shard_map/all_to_all | solution.py:417
  93.7 6.0 %all_gather.3.sums_ref = bf16[1536,128]{1,0:T(8,128)(2,1)S(1)} all-gather(bf16[768,128]{1,0:T(8,128)(2,1)S(1)} %bitcast.21), channel_id=1, replica_groups=mesh['yh'=4,'z'=8,'gy'=8,'gx'=2] {'gx'}, dimensions={0}, use_global_device_ids=true | all-gather | bytes 589824 | tf_op jit(solution)/shard_map/all_gather | solution.py:441
  99.8 1.2 %finish.1 = (f32[192]{0:T(256)}, f32[192]{0:T(256)}, f32[192,576]{1,0:T(8,128)}, f32[576]{0:T(1024)}, f32[192,192]{1,0:T(8,128)}, /*index=5*/f32[6,1575]{1,0:T(8,128)}) custom-call(bf16[1536,128]{1,0:T(8,128)(2,1)S(1)} %all_gather.3.sums_ref), custom_call_target="tpu_custom_call" | custom-call | tf_op jit(solution)/shard_map/finish/pallas_call | solution.py:328
  101.0 0.8 fusion
  (39 shorter events, 1.9 us)
Async XLA Ops:
  1.9 26.1 %collective-permute-start = (bf16[2,4,16,384]{3,2,1,0:T(8,128)(2,1)S(1)}, bf16[2,4,16,384]{3,2,1,0:T(8,128)(2,1)S(1)}, u32[]{:S(2)}, u32[]{:S(2)}) collective-permute-start(bf16[2,4,16,384]{3,2,1,0:T(8,128)(2,1)S(1)} %get-tuple-element.48), channel_id=1, source_target_pairs={{0,496},{16,0},{32,16},{48,32},{64,48},{80,64},{96,80},{112,96},{1... | collective-permute-start | bytes 294920 | tf_op jit(solution)/shard_map/ppermute | solution.py:386
  17.1 7.0 %copy-start.5 = (f32[576]{0:T(1024)S(1)}, f32[576]{0:T(1024)}, u32[]{:S(2)}) copy-start(f32[576]{0:T(1024)} %param.12) | copy-start | bytes 6916
  17.1 11.0 %collective-permute-start.1 = (bf16[2,4,16,384]{3,2,1,0:T(8,128)(2,1)S(1)}, bf16[2,4,16,384]{3,2,1,0:T(8,128)(2,1)S(1)}, u32[]{:S(2)}, u32[]{:S(2)}) collective-permute-start(bf16[2,4,16,384]{3,2,1,0:T(8,128)(2,1)S(1)} %get-tuple-element.49), channel_id=1, source_target_pairs={{0,510},{2,496},{4,498},{6,500},{8,502},{10,504},{12,506},{14,508}... | collective-permute-start | bytes 294920 | tf_op jit(solution)/shard_map/ppermute | solution.py:386
  20.7 7.4 %collective-permute-start.2 = (bf16[2,4,16,384]{3,2,1,0:T(8,128)(2,1)S(1)}, bf16[2,4,16,384]{3,2,1,0:T(8,128)(2,1)S(1)}, u32[]{:S(2)}, u32[]{:S(2)}) collective-permute-start(bf16[2,4,16,384]{3,2,1,0:T(8,128)(2,1)S(1)} %get-tuple-element.50), channel_id=1, source_target_pairs={{0,14},{2,0},{4,2},{6,4},{8,6},{10,8},{12,10},{14,12},{1,15},{3,1}... | collective-permute-start | bytes 294920 | tf_op jit(solution)/shard_map/ppermute | solution.py:386
  24.1 0.8 copy-start.4
  25.8 1.0 copy-start.3
  27.1 0.7 copy-start.7
  27.1 1.0 copy-start.1
  27.1 1.0 %copy-start.2 = (bf16[4,8,16,192]{3,2,1,0:T(8,128)(2,1)S(1)}, bf16[4,8,16,192]{3,2,1,0:T(8,128)(2,1)}, u32[]{:S(2)}) copy-start(bf16[4,8,16,192]{3,2,1,0:T(8,128)(2,1)} %param.15) | copy-start | bytes 589828
  27.3 0.7 copy-start.6
  28.1 4.4 %copy-start = (bf16[192,192]{1,0:T(8,128)(2,1)S(1)}, bf16[192,192]{1,0:T(8,128)(2,1)}, u32[]{:S(2)}) copy-start(bf16[192,192]{1,0:T(8,128)(2,1)} %proj_ref.1) | copy-start | bytes 221188
  28.2 4.4 %collective-permute-start.3 = (bf16[4,8,4,384]{3,2,1,0:T(4,128)(2,1)S(1)}, bf16[4,8,4,384]{3,2,1,0:T(4,128)(2,1)S(1)}, u32[]{:S(2)}, u32[]{:S(2)}) collective-permute-start(bf16[4,8,4,384]{3,2,1,0:T(4,128)(2,1)S(1)} %fusion.9), channel_id=1, source_target_pairs={{0,1},{1,0},{2,3},{3,2},{4,5},{5,4},{6,7},{7,6},{8,9},{9,8},{10,11... | collective-permute-start | bytes 294920 | tf_op jit(solution)/shard_map/ppermute | solution.py:386
  40.6 3.6 %collective-permute-start.4 = (f32[768,128]{1,0:T(8,128)S(1)}, f32[768,128]{1,0:T(8,128)S(1)}, u32[]{:S(2)}, u32[]{:S(2)}) collective-permute-start(f32[768,128]{1,0:T(8,128)S(1)} %constant_dynamic-slice_fusion), channel_id=1, source_target_pairs={{0,1},{1,0},{2,3},{3,2},{4,5},{5,4},{6,7},{7,6},{8,9},{9,8},{10,11... | collective-permute-start | bytes 1179656 | tf_op jit(solution)/shard_map/ppermute | solution.py:411
  45.0 21.2 %all-to-all-start = ((f32[32,24,128]{2,1,0:T(8,128)}), f32[32,24,128]{2,1,0:T(8,128)S(1)}, u32[]{:S(2)}, u32[]{:S(2)}) async-start(f32[32,24,128]{2,1,0:T(8,128)} %bitcast.10), calls=%async_computation | async-start | bytes 786432 | tf_op jit(solution)/shard_map/all_to_all | solution.py:434
  52.4 3.5 %collective-permute-start.5 = (bf16[4,8,8,192]{3,2,1,0:T(8,128)(2,1)S(1)}, bf16[4,8,8,192]{3,2,1,0:T(8,128)(2,1)S(1)}, u32[]{:S(2)}, u32[]{:S(2)}) collective-permute-start(bf16[4,8,8,192]{3,2,1,0:T(8,128)(2,1)S(1)} %get-tuple-element.28), channel_id=1, source_target_pairs={{0,1},{1,0},{2,3},{3,2},{4,5},{5,4},{6,7},{7,6},{8,9},{9,8},{10,11... | collective-permute-start | bytes 294920 | tf_op jit(solution)/shard_map/ppermute | solution.py:386
  67.0 11.0 %all-to-all-start.1 = ((f32[8,24,128]{2,1,0:T(8,128)}), f32[8,24,128]{2,1,0:T(8,128)S(1)}, u32[]{:S(2)}, u32[]{:S(2)}) async-start(f32[8,24,128]{2,1,0:T(8,128)} %broadcast_in_dim.4), calls=%async_computation.1 | async-start | bytes 196608 | tf_op jit(solution)/shard_map/all_to_all | solution.py:417
  70.5 7.8 %collective-permute-start.6 = (bf16[4,4,16,192]{3,2,1,0:T(8,128)(2,1)S(1)}, bf16[4,4,16,192]{3,2,1,0:T(8,128)(2,1)S(1)}, u32[]{:S(2)}, u32[]{:S(2)}) collective-permute-start(bf16[4,4,16,192]{3,2,1,0:T(8,128)(2,1)S(1)} %fusion.4), channel_id=1, source_target_pairs={{0,2},{2,4},{4,6},{6,8},{8,10},{10,12},{12,14},{14,0},{1,3},{3,5},... | collective-permute-start | bytes 294920 | tf_op jit(solution)/shard_map/ppermute | solution.py:386
  79.0 14.7 %all-to-all-start.2 = ((bf16[32,24,128]{2,1,0:T(8,128)(2,1)}), bf16[32,24,128]{2,1,0:T(8,128)(2,1)S(1)}, u32[]{:S(2)}, u32[]{:S(2)}) async-start(bf16[32,24,128]{2,1,0:T(8,128)(2,1)} %broadcast_in_dim.5), calls=%async_computation.2 | async-start | bytes 393216 | tf_op jit(solution)/shard_map/all_to_all | solution.py:417
  83.9 17.1 %collective-permute-start.7 = (bf16[2,8,16,192]{3,2,1,0:T(8,128)(2,1)S(1)}, bf16[2,8,16,192]{3,2,1,0:T(8,128)(2,1)S(1)}, u32[]{:S(2)}, u32[]{:S(2)}) collective-permute-start(bf16[2,8,16,192]{3,2,1,0:T(8,128)(2,1)S(1)} %fusion.5), channel_id=1, source_target_pairs={{0,16},{16,32},{32,48},{48,64},{64,80},{80,96},{96,112},{112,128},... | collective-permute-start | bytes 294920 | tf_op jit(solution)/shard_map/ppermute | solution.py:386

commit v4 on v3

--- a/solution.py
+++ b/solution.py
@@ -426,14 +426,15 @@
     core = lax.axis_index("gx")
     mine = lax.dynamic_slice_in_dim(sums, core * half, half, 0)
     other = lax.dynamic_slice_in_dim(sums, (1 - core) * half, half, 0)
-    mine = mine + swapped(other, "gx", (1, 0))
+    mine = (mine + swapped(other, "gx", (1, 0))).astype(BF16)
     border = sent(border, gx=1)[:, :, :SX]
     field = jnp.concatenate([border, field[:, :, SX:]], 2)
     y_border = sent(field[:, SY:], gy=1)
     count = lax.axis_size(PLANE)
-    part = lax.all_to_all(mine.reshape(count, half // count, 128), PLANE, 0, 0, tiled=True).sum(0)
+    part = lax.all_to_all(mine.reshape(count, half // count, 128), PLANE, 0, 0, tiled=True)
+    part = part.astype(F32).sum(0)
     part, field = after(part, field)
-    part = to_each(part, "z").sum(0).astype(BF16)
+    part = to_each(part, "z").sum(0)
     part, y_border = after(part, y_border)
     field = jnp.concatenate([y_border, field[:, :SY]], 1)
     z_border = sent(field[SZ:], gz=1)

time: 103 us -> 101 us (0.981)
  starting transfers between devices: 52 us -> 50.1 us
    all_to_all x1, waiting for transfers between devices: 10.2 us -> 6.91 us  [unshift_and_reduce(): lax.all_to_all(mine.reshape(count, half // count, 128), PLANE, 0, 0, tile...]
    all_to_all x2, waiting for transfers between devices: 11.3 us -> 14.3 us  [to_each(): return lax.all_to_all(spread, axes, 0, 0, tiled=True)]
where the time goes in v4:
time: 101 us
  starting transfers between devices  50.1 us (50%)
  waiting for transfers between devices  24.7 us (24%)
  Pallas kernels  9.24 us (9%)
  blocking collectives  7.02 us (7%)
  local copies, waits for them, and re-layouts  5.46 us (5%)
  other arithmetic  3.13 us (3%)
    ppermute x7, starting transfers between devices, sent(): return lax.ppermute(value, tuple(axes), pairs)  33.1 us
    all_to_all x2, waiting for transfers between devices, to_each(): return lax.all_to_all(spread, axes, 0, 0, tiled=True)  14.3 us
    pallas_call x1, Pallas kernels, windows(): pl.pallas_call(functools.partial(kernel, scale), out_shape=(jax.ShapeDtyp...  8.01 us
    all_to_all x1, starting transfers between devices, unshift_and_reduce(): lax.all_to_all(mine.reshape(count, half // count, 128), PLANE, 0, 0, tile...  7.35 us
    all_to_all x2, starting transfers between devices, to_each(): return lax.all_to_all(spread, axes, 0, 0, tiled=True)  7.32 us
    all_gather x1, blocking collectives, unshift_and_reduce(): outputs = finish(lax.all_gather(mine, 'gx', axis=0, tiled=True))  7.02 us
    all_to_all x1, waiting for transfers between devices, unshift_and_reduce(): lax.all_to_all(mine.reshape(count, half // count, 128), PLANE, 0, 0, tile...  6.91 us
    ppermute x1, starting transfers between devices, swapped(): return lax.ppermute(value, axis, list(enumerate(partners)))  2.26 us
  transfers between devices with their start and end apart: 11, of which 7 were waited for; matrix products, arithmetic and copies ran while one was open for 2% of the time, Pallas kernels for 1%

profile of v4, /device:TPU:1, one launch (start us, length us, event | category | flops | bytes accessed | tf_op | source)
XLA Modules:
  0.0 100.6 jit_solution(17913095685052914373)
XLA Ops:
  0.6 1.2 %fusion.11 = (bf16[2,4,16,384]{3,2,1,0:T(8,128)(2,1)S(1)}, bf16[2,4,16,384]{3,2,1,0:T(8,128)(2,1)S(1)}, bf16[2,4,16,384]{3,2,1,0:T(8,128)(2,1)S(1)}, bf16[2,4,16,384]{3,2,1,0:T(8,128)(2,1)S(1)}) fusion(bf16[4,8,16,192]{3,2,1,0:T(8,128)(2,1)} %param.8, bf16[4,8,16,192]{3,2,1,0:T(8,128)(2,1)} %param.15), kind=kLoop, calls=%fused_computation.29 | loop fusion | flops 786432 | bytes 786432 | tf_op jit(solution)/shard_map/concatenate | solution.py:390
  1.9 15.2 %collective-permute-start = (bf16[2,4,16,384]{3,2,1,0:T(8,128)(2,1)S(1)}, bf16[2,4,16,384]{3,2,1,0:T(8,128)(2,1)S(1)}, u32[]{:S(2)}, u32[]{:S(2)}) collective-permute-start(bf16[2,4,16,384]{3,2,1,0:T(8,128)(2,1)S(1)} %get-tuple-element.48), channel_id=1, source_target_pairs={{0,496},{16,0},{32,16},{48,32},{64,48},{80,64},{96,80},{112,96},{1... | collective-permute-start | bytes 294920 | tf_op jit(solution)/shard_map/ppermute | solution.py:386
  17.1 3.6 %collective-permute-start.1 = (bf16[2,4,16,384]{3,2,1,0:T(8,128)(2,1)S(1)}, bf16[2,4,16,384]{3,2,1,0:T(8,128)(2,1)S(1)}, u32[]{:S(2)}, u32[]{:S(2)}) collective-permute-start(bf16[2,4,16,384]{3,2,1,0:T(8,128)(2,1)S(1)} %get-tuple-element.49), channel_id=1, source_target_pairs={{0,510},{2,496},{4,498},{6,500},{8,502},{10,504},{12,506},{14,508}... | collective-permute-start | bytes 294920 | tf_op jit(solution)/shard_map/ppermute | solution.py:386
  20.7 3.4 %collective-permute-start.2 = (bf16[2,4,16,384]{3,2,1,0:T(8,128)(2,1)S(1)}, bf16[2,4,16,384]{3,2,1,0:T(8,128)(2,1)S(1)}, u32[]{:S(2)}, u32[]{:S(2)}) collective-permute-start(bf16[2,4,16,384]{3,2,1,0:T(8,128)(2,1)S(1)} %get-tuple-element.50), channel_id=1, source_target_pairs={{0,14},{2,0},{4,2},{6,4},{8,6},{10,8},{12,10},{14,12},{1,15},{3,1}... | collective-permute-start | bytes 294920 | tf_op jit(solution)/shard_map/ppermute | solution.py:386
  24.1 0.2 reshape.52.qkv_bias_t_ref
  24.4 0.5 copy-done.4
  25.2 0.5 reshape.48
  25.8 0.4 reshape.49.table_ref
  26.2 0.5 copy-done.3
  27.3 0.5 copy-done.7
  28.2 3.4 %collective-permute-start.3 = (bf16[4,8,4,384]{3,2,1,0:T(4,128)(2,1)S(1)}, bf16[4,8,4,384]{3,2,1,0:T(4,128)(2,1)S(1)}, u32[]{:S(2)}, u32[]{:S(2)}) collective-permute-start(bf16[4,8,4,384]{3,2,1,0:T(4,128)(2,1)S(1)} %fusion.9), channel_id=1, source_target_pairs={{0,1},{1,0},{2,3},{3,2},{4,5},{5,4},{6,7},{7,6},{8,9},{9,8},{10,11... | collective-permute-start | bytes 294920 | tf_op jit(solution)/shard_map/ppermute | solution.py:386
  31.7 0.8 collective-permute-done.3.border_ref
  32.6 8.0 %windows.1 = (bf16[4,8,16,192]{3,2,1,0:T(8,128)(2,1)S(1)}, bf16[4,8,8,192]{3,2,1,0:T(8,128)(2,1)S(1)}, f32[1536,128]{1,0:T(8,128)S(1)}) custom-call(s32[3]{0:T(128)S(1)} %add_convert_fusion.1.flags_ref, bf16[2,4,16,384]{3,2,1,0:T(8,128)(2,1)S(1)} %collective-permute-done.z_ref, bf16[2,4,16,384]{3,2,1,0:T(8,128)(2,1)S(1)} %collective-permute-done.1.zy_ref, ...), custom_call_target="tpu_custom_call" | custom-call | flops 1000000000 | bytes 3000000 | tf_op jit(solution)/shard_map/windows/pallas_call | solution.py:343
  40.6 2.3 %collective-permute-start.4 = (f32[768,128]{1,0:T(8,128)S(1)}, f32[768,128]{1,0:T(8,128)S(1)}, u32[]{:S(2)}, u32[]{:S(2)}) collective-permute-start(f32[768,128]{1,0:T(8,128)S(1)} %constant_dynamic-slice_fusion), channel_id=1, source_target_pairs={{0,1},{1,0},{2,3},{3,2},{4,5},{5,4},{6,7},{7,6},{8,9},{9,8},{10,11... | collective-permute-start | bytes 1179656 | tf_op jit(solution)/shard_map/ppermute | solution.py:411
  42.9 1.3 %collective-permute-done.4 = f32[768,128]{1,0:T(8,128)S(1)} collective-permute-done((f32[768,128]{1,0:T(8,128)S(1)}, f32[768,128]{1,0:T(8,128)S(1)}, u32[]{:S(2)}, u32[]{:S(2)}) %collective-permute-start.4) | collective-permute-done | bytes 393248 | tf_op jit(solution)/shard_map/ppermute | solution.py:411
  44.3 0.7 add_convert_fusion
  45.0 7.3 %all-to-all-start = ((bf16[32,24,128]{2,1,0:T(8,128)(2,1)}), bf16[32,24,128]{2,1,0:T(8,128)(2,1)S(1)}, u32[]{:S(2)}, u32[]{:S(2)}) async-start(bf16[32,24,128]{2,1,0:T(8,128)(2,1)} %bitcast.10), calls=%async_computation | async-start | bytes 393216 | tf_op jit(solution)/shard_map/all_to_all | solution.py:434
  52.3 2.5 %collective-permute-start.5 = (bf16[4,8,8,192]{3,2,1,0:T(8,128)(2,1)S(1)}, bf16[4,8,8,192]{3,2,1,0:T(8,128)(2,1)S(1)}, u32[]{:S(2)}, u32[]{:S(2)}) collective-permute-start(bf16[4,8,8,192]{3,2,1,0:T(8,128)(2,1)S(1)} %get-tuple-element.28), channel_id=1, source_target_pairs={{0,1},{1,0},{2,3},{3,2},{4,5},{5,4},{6,7},{7,6},{8,9},{9,8},{10,11... | collective-permute-start | bytes 294920 | tf_op jit(solution)/shard_map/ppermute | solution.py:386
  55.0 0.9 collective-permute-done.5
  56.0 6.9 %all-to-all-done = bf16[32,24,128]{2,1,0:T(8,128)(2,1)S(1)} async-done(((bf16[32,24,128]{2,1,0:T(8,128)(2,1)}), bf16[32,24,128]{2,1,0:T(8,128)(2,1)S(1)}, u32[]{:S(2)}, u32[]{:S(2)}) %all-to-all-start) | async-done | bytes 196640 | tf_op jit(solution)/shard_map/all_to_all | solution.py:434
  62.9 0.6 broadcast_in_dim.4
  63.6 3.4 %all-to-all-start.1 = ((f32[8,24,128]{2,1,0:T(8,128)}), f32[8,24,128]{2,1,0:T(8,128)S(1)}, u32[]{:S(2)}, u32[]{:S(2)}) async-start(f32[8,24,128]{2,1,0:T(8,128)} %broadcast_in_dim.4), calls=%async_computation.1 | async-start | bytes 196608 | tf_op jit(solution)/shard_map/all_to_all | solution.py:417
  67.1 1.9 %collective-permute-start.6 = (bf16[4,4,16,192]{3,2,1,0:T(8,128)(2,1)S(1)}, bf16[4,4,16,192]{3,2,1,0:T(8,128)(2,1)S(1)}, u32[]{:S(2)}, u32[]{:S(2)}) collective-permute-start(bf16[4,4,16,192]{3,2,1,0:T(8,128)(2,1)S(1)} %fusion.4), channel_id=1, source_target_pairs={{0,2},{2,4},{4,6},{6,8},{8,10},{10,12},{12,14},{14,0},{1,3},{3,5},... | collective-permute-start | bytes 294920 | tf_op jit(solution)/shard_map/ppermute | solution.py:386
  69.0 5.7 %all-to-all-done.1 = f32[8,24,128]{2,1,0:T(8,128)S(1)} async-done(((f32[8,24,128]{2,1,0:T(8,128)}), f32[8,24,128]{2,1,0:T(8,128)S(1)}, u32[]{:S(2)}, u32[]{:S(2)}) %all-to-all-start.1) | async-done | bytes 98336 | tf_op jit(solution)/shard_map/all_to_all | solution.py:417
  74.7 0.4 collective-permute-done.6
  75.2 0.8 broadcast_in_dim.5
  75.9 3.9 %all-to-all-start.2 = ((f32[32,24,128]{2,1,0:T(8,128)}), f32[32,24,128]{2,1,0:T(8,128)S(1)}, u32[]{:S(2)}, u32[]{:S(2)}) async-start(f32[32,24,128]{2,1,0:T(8,128)} %broadcast_in_dim.5), calls=%async_computation.2 | async-start | bytes 786432 | tf_op jit(solution)/shard_map/all_to_all | solution.py:417
  79.9 3.1 %collective-permute-start.7 = (bf16[2,8,16,192]{3,2,1,0:T(8,128)(2,1)S(1)}, bf16[2,8,16,192]{3,2,1,0:T(8,128)(2,1)S(1)}, u32[]{:S(2)}, u32[]{:S(2)}) collective-permute-start(bf16[2,8,16,192]{3,2,1,0:T(8,128)(2,1)S(1)} %fusion.5), channel_id=1, source_target_pairs={{0,16},{16,32},{32,48},{48,64},{64,80},{80,96},{96,112},{112,128},... | collective-permute-start | bytes 294920 | tf_op jit(solution)/shard_map/ppermute | solution.py:386
  83.0 8.6 %all-to-all-done.2 = f32[32,24,128]{2,1,0:T(8,128)S(1)} async-done(((f32[32,24,128]{2,1,0:T(8,128)}), f32[32,24,128]{2,1,0:T(8,128)S(1)}, u32[]{:S(2)}, u32[]{:S(2)}) %all-to-all-start.2) | async-done | bytes 393248 | tf_op jit(solution)/shard_map/all_to_all | solution.py:417
  91.6 7.0 %all_gather.3.sums_ref = f32[1536,128]{1,0:T(8,128)S(1)} all-gather(f32[768,128]{1,0:T(8,128)S(1)} %bitcast.19), channel_id=1, replica_groups=mesh['yh'=4,'z'=8,'gy'=8,'gx'=2] {'gx'}, dimensions={0}, use_global_device_ids=true | all-gather | bytes 1179648 | tf_op jit(solution)/shard_map/all_gather | solution.py:442
  98.6 1.2 %finish.1 = (f32[192]{0:T(256)}, f32[192]{0:T(256)}, f32[192,576]{1,0:T(8,128)}, f32[576]{0:T(1024)}, f32[192,192]{1,0:T(8,128)}, /*index=5*/f32[6,1575]{1,0:T(8,128)}) custom-call(f32[1536,128]{1,0:T(8,128)S(1)} %all_gather.3.sums_ref), custom_call_target="tpu_custom_call" | custom-call | tf_op jit(solution)/shard_map/finish/pallas_call | solution.py:328
  99.8 0.8 fusion
  (39 shorter events, 1.9 us)
Async XLA Ops:
  1.9 26.1 %collective-permute-start = (bf16[2,4,16,384]{3,2,1,0:T(8,128)(2,1)S(1)}, bf16[2,4,16,384]{3,2,1,0:T(8,128)(2,1)S(1)}, u32[]{:S(2)}, u32[]{:S(2)}) collective-permute-start(bf16[2,4,16,384]{3,2,1,0:T(8,128)(2,1)S(1)} %get-tuple-element.48), channel_id=1, source_target_pairs={{0,496},{16,0},{32,16},{48,32},{64,48},{80,64},{96,80},{112,96},{1... | collective-permute-start | bytes 294920 | tf_op jit(solution)/shard_map/ppermute | solution.py:386
  17.1 7.0 %copy-start.5 = (f32[576]{0:T(1024)S(1)}, f32[576]{0:T(1024)}, u32[]{:S(2)}) copy-start(f32[576]{0:T(1024)} %param.12) | copy-start | bytes 6916
  17.1 11.0 %collective-permute-start.1 = (bf16[2,4,16,384]{3,2,1,0:T(8,128)(2,1)S(1)}, bf16[2,4,16,384]{3,2,1,0:T(8,128)(2,1)S(1)}, u32[]{:S(2)}, u32[]{:S(2)}) collective-permute-start(bf16[2,4,16,384]{3,2,1,0:T(8,128)(2,1)S(1)} %get-tuple-element.49), channel_id=1, source_target_pairs={{0,510},{2,496},{4,498},{6,500},{8,502},{10,504},{12,506},{14,508}... | collective-permute-start | bytes 294920 | tf_op jit(solution)/shard_map/ppermute | solution.py:386
  20.7 7.4 %collective-permute-start.2 = (bf16[2,4,16,384]{3,2,1,0:T(8,128)(2,1)S(1)}, bf16[2,4,16,384]{3,2,1,0:T(8,128)(2,1)S(1)}, u32[]{:S(2)}, u32[]{:S(2)}) collective-permute-start(bf16[2,4,16,384]{3,2,1,0:T(8,128)(2,1)S(1)} %get-tuple-element.50), channel_id=1, source_target_pairs={{0,14},{2,0},{4,2},{6,4},{8,6},{10,8},{12,10},{14,12},{1,15},{3,1}... | collective-permute-start | bytes 294920 | tf_op jit(solution)/shard_map/ppermute | solution.py:386
  24.1 0.8 copy-start.4
  25.8 1.0 copy-start.3
  27.1 0.7 copy-start.7
  27.1 1.0 copy-start.1
  27.1 1.0 %copy-start.2 = (bf16[4,8,16,192]{3,2,1,0:T(8,128)(2,1)S(1)}, bf16[4,8,16,192]{3,2,1,0:T(8,128)(2,1)}, u32[]{:S(2)}) copy-start(bf16[4,8,16,192]{3,2,1,0:T(8,128)(2,1)} %param.15) | copy-start | bytes 589828
  27.3 0.7 copy-start.6
  28.1 4.4 %copy-start = (bf16[192,192]{1,0:T(8,128)(2,1)S(1)}, bf16[192,192]{1,0:T(8,128)(2,1)}, u32[]{:S(2)}) copy-start(bf16[192,192]{1,0:T(8,128)(2,1)} %proj_ref.1) | copy-start | bytes 221188
  28.2 4.4 %collective-permute-start.3 = (bf16[4,8,4,384]{3,2,1,0:T(4,128)(2,1)S(1)}, bf16[4,8,4,384]{3,2,1,0:T(4,128)(2,1)S(1)}, u32[]{:S(2)}, u32[]{:S(2)}) collective-permute-start(bf16[4,8,4,384]{3,2,1,0:T(4,128)(2,1)S(1)} %fusion.9), channel_id=1, source_target_pairs={{0,1},{1,0},{2,3},{3,2},{4,5},{5,4},{6,7},{7,6},{8,9},{9,8},{10,11... | collective-permute-start | bytes 294920 | tf_op jit(solution)/shard_map/ppermute | solution.py:386
  40.6 3.6 %collective-permute-start.4 = (f32[768,128]{1,0:T(8,128)S(1)}, f32[768,128]{1,0:T(8,128)S(1)}, u32[]{:S(2)}, u32[]{:S(2)}) collective-permute-start(f32[768,128]{1,0:T(8,128)S(1)} %constant_dynamic-slice_fusion), channel_id=1, source_target_pairs={{0,1},{1,0},{2,3},{3,2},{4,5},{5,4},{6,7},{7,6},{8,9},{9,8},{10,11... | collective-permute-start | bytes 1179656 | tf_op jit(solution)/shard_map/ppermute | solution.py:411
  45.0 17.9 %all-to-all-start = ((bf16[32,24,128]{2,1,0:T(8,128)(2,1)}), bf16[32,24,128]{2,1,0:T(8,128)(2,1)S(1)}, u32[]{:S(2)}, u32[]{:S(2)}) async-start(bf16[32,24,128]{2,1,0:T(8,128)(2,1)} %bitcast.10), calls=%async_computation | async-start | bytes 393216 | tf_op jit(solution)/shard_map/all_to_all | solution.py:434
  52.3 3.5 %collective-permute-start.5 = (bf16[4,8,8,192]{3,2,1,0:T(8,128)(2,1)S(1)}, bf16[4,8,8,192]{3,2,1,0:T(8,128)(2,1)S(1)}, u32[]{:S(2)}, u32[]{:S(2)}) collective-permute-start(bf16[4,8,8,192]{3,2,1,0:T(8,128)(2,1)S(1)} %get-tuple-element.28), channel_id=1, source_target_pairs={{0,1},{1,0},{2,3},{3,2},{4,5},{5,4},{6,7},{7,6},{8,9},{9,8},{10,11... | collective-permute-start | bytes 294920 | tf_op jit(solution)/shard_map/ppermute | solution.py:386
  63.6 11.1 %all-to-all-start.1 = ((f32[8,24,128]{2,1,0:T(8,128)}), f32[8,24,128]{2,1,0:T(8,128)S(1)}, u32[]{:S(2)}, u32[]{:S(2)}) async-start(f32[8,24,128]{2,1,0:T(8,128)} %broadcast_in_dim.4), calls=%async_computation.1 | async-start | bytes 196608 | tf_op jit(solution)/shard_map/all_to_all | solution.py:417
  67.1 8.1 %collective-permute-start.6 = (bf16[4,4,16,192]{3,2,1,0:T(8,128)(2,1)S(1)}, bf16[4,4,16,192]{3,2,1,0:T(8,128)(2,1)S(1)}, u32[]{:S(2)}, u32[]{:S(2)}) collective-permute-start(bf16[4,4,16,192]{3,2,1,0:T(8,128)(2,1)S(1)} %fusion.4), channel_id=1, source_target_pairs={{0,2},{2,4},{4,6},{6,8},{8,10},{10,12},{12,14},{14,0},{1,3},{3,5},... | collective-permute-start | bytes 294920 | tf_op jit(solution)/shard_map/ppermute | solution.py:386
  75.9 15.6 %all-to-all-start.2 = ((f32[32,24,128]{2,1,0:T(8,128)}), f32[32,24,128]{2,1,0:T(8,128)S(1)}, u32[]{:S(2)}, u32[]{:S(2)}) async-start(f32[32,24,128]{2,1,0:T(8,128)} %broadcast_in_dim.5), calls=%async_computation.2 | async-start | bytes 786432 | tf_op jit(solution)/shard_map/all_to_all | solution.py:417
  79.9 20.0 %collective-permute-start.7 = (bf16[2,8,16,192]{3,2,1,0:T(8,128)(2,1)S(1)}, bf16[2,8,16,192]{3,2,1,0:T(8,128)(2,1)S(1)}, u32[]{:S(2)}, u32[]{:S(2)}) collective-permute-start(bf16[2,8,16,192]{3,2,1,0:T(8,128)(2,1)S(1)} %fusion.5), channel_id=1, source_target_pairs={{0,16},{16,32},{32,48},{48,64},{64,80},{80,96},{96,112},{112,128},... | collective-permute-start | bytes 294920 | tf_op jit(solution)/shard_map/ppermute | solution.py:386

commit v5 on v4

--- a/solution.py
+++ b/solution.py
@@ -427,7 +427,7 @@
     mine = lax.dynamic_slice_in_dim(sums, core * half, half, 0)
     other = lax.dynamic_slice_in_dim(sums, (1 - core) * half, half, 0)
     mine = (mine + swapped(other, "gx", (1, 0))).astype(BF16)
-    border = sent(border, gx=1)[:, :, :SX]
+    mine, border = after(mine, sent(border, gx=1)[:, :, :SX])
     field = jnp.concatenate([border, field[:, :, SX:]], 2)
     y_border = sent(field[:, SY:], gy=1)
     count = lax.axis_size(PLANE)

time: 101 us -> 103 us (1.020)
  waiting for transfers between devices: 24.7 us -> 27.1 us
    all_to_all x1, waiting for transfers between devices: 6.91 us -> 10.4 us  [unshift_and_reduce(): lax.all_to_all(mine.reshape(count, half // count, 128), PLANE, 0, 0, tile...]
    ppermute x1, waiting for transfers between devices: 1.34 us -> 0.01 us  [swapped(): return lax.ppermute(value, axis, list(enumerate(partners)))]
  transfers between devices with their start and end apart: 11 -> 11, of which waited for: 7 -> 6; matrix products, arithmetic and copies ran while one was open for 2% -> 2% of each run, Pallas kernels for 1% -> 1%
where the time goes in v5:
time: 103 us
  starting transfers between devices  49.6 us (48%)
  waiting for transfers between devices  27.1 us (26%)
  Pallas kernels  9.24 us (9%)
  blocking collectives  7.02 us (7%)
  local copies, waits for them, and re-layouts  5.46 us (5%)
  other arithmetic  3.14 us (3%)
    ppermute x7, starting transfers between devices, sent(): return lax.ppermute(value, tuple(axes), pairs)  32.7 us
    all_to_all x2, waiting for transfers between devices, to_each(): return lax.all_to_all(spread, axes, 0, 0, tiled=True)  14.2 us
    all_to_all x1, waiting for transfers between devices, unshift_and_reduce(): lax.all_to_all(mine.reshape(count, half // count, 128), PLANE, 0, 0, tile...  10.4 us
    pallas_call x1, Pallas kernels, windows(): pl.pallas_call(functools.partial(kernel, scale), out_shape=(jax.ShapeDtyp...  8.01 us
    all_to_all x1, starting transfers between devices, unshift_and_reduce(): lax.all_to_all(mine.reshape(count, half // count, 128), PLANE, 0, 0, tile...  7.35 us
    all_to_all x2, starting transfers between devices, to_each(): return lax.all_to_all(spread, axes, 0, 0, tiled=True)  7.34 us
    all_gather x1, blocking collectives, unshift_and_reduce(): outputs = finish(lax.all_gather(mine, 'gx', axis=0, tiled=True))  7.02 us
    ppermute x7, waiting for transfers between devices, sent(): return lax.ppermute(value, tuple(axes), pairs)  2.56 us
  transfers between devices with their start and end apart: 11, of which 6 were waited for; matrix products, arithmetic and copies ran while one was open for 2% of the time, Pallas kernels for 1%

profile of v5, /device:TPU:1, one launch (start us, length us, event | category | flops | bytes accessed | tf_op | source)
XLA Modules:
  0.0 102.6 jit_solution(5007255502949625812)
XLA Ops:
  0.6 1.2 %fusion.11 = (bf16[2,4,16,384]{3,2,1,0:T(8,128)(2,1)S(1)}, bf16[2,4,16,384]{3,2,1,0:T(8,128)(2,1)S(1)}, bf16[2,4,16,384]{3,2,1,0:T(8,128)(2,1)S(1)}, bf16[2,4,16,384]{3,2,1,0:T(8,128)(2,1)S(1)}) fusion(bf16[4,8,16,192]{3,2,1,0:T(8,128)(2,1)} %param.8, bf16[4,8,16,192]{3,2,1,0:T(8,128)(2,1)} %param.15), kind=kLoop, calls=%fused_computation.29 | loop fusion | flops 786432 | bytes 786432 | tf_op jit(solution)/shard_map/concatenate | solution.py:390
  1.9 15.2 %collective-permute-start = (bf16[2,4,16,384]{3,2,1,0:T(8,128)(2,1)S(1)}, bf16[2,4,16,384]{3,2,1,0:T(8,128)(2,1)S(1)}, u32[]{:S(2)}, u32[]{:S(2)}) collective-permute-start(bf16[2,4,16,384]{3,2,1,0:T(8,128)(2,1)S(1)} %get-tuple-element.52), channel_id=1, source_target_pairs={{0,496},{16,0},{32,16},{48,32},{64,48},{80,64},{96,80},{112,96},{1... | collective-permute-start | bytes 294920 | tf_op jit(solution)/shard_map/ppermute | solution.py:386
  17.1 3.6 %collective-permute-start.1 = (bf16[2,4,16,384]{3,2,1,0:T(8,128)(2,1)S(1)}, bf16[2,4,16,384]{3,2,1,0:T(8,128)(2,1)S(1)}, u32[]{:S(2)}, u32[]{:S(2)}) collective-permute-start(bf16[2,4,16,384]{3,2,1,0:T(8,128)(2,1)S(1)} %get-tuple-element.53), channel_id=1, source_target_pairs={{0,510},{2,496},{4,498},{6,500},{8,502},{10,504},{12,506},{14,508}... | collective-permute-start | bytes 294920 | tf_op jit(solution)/shard_map/ppermute | solution.py:386
  20.7 3.4 %collective-permute-start.2 = (bf16[2,4,16,384]{3,2,1,0:T(8,128)(2,1)S(1)}, bf16[2,4,16,384]{3,2,1,0:T(8,128)(2,1)S(1)}, u32[]{:S(2)}, u32[]{:S(2)}) collective-permute-start(bf16[2,4,16,384]{3,2,1,0:T(8,128)(2,1)S(1)} %get-tuple-element.54), channel_id=1, source_target_pairs={{0,14},{2,0},{4,2},{6,4},{8,6},{10,8},{12,10},{14,12},{1,15},{3,1}... | collective-permute-start | bytes 294920 | tf_op jit(solution)/shard_map/ppermute | solution.py:386
  24.1 0.2 reshape.52.qkv_bias_t_ref
  24.4 0.5 copy-done.4
  25.2 0.5 reshape.48
  25.8 0.4 reshape.49.table_ref
  26.2 0.5 copy-done.3
  27.3 0.5 copy-done.7
  27.8 0.2 copy-done.6
  28.2 3.4 %collective-permute-start.3 = (bf16[4,8,4,384]{3,2,1,0:T(4,128)(2,1)S(1)}, bf16[4,8,4,384]{3,2,1,0:T(4,128)(2,1)S(1)}, u32[]{:S(2)}, u32[]{:S(2)}) collective-permute-start(bf16[4,8,4,384]{3,2,1,0:T(4,128)(2,1)S(1)} %fusion.9), channel_id=1, source_target_pairs={{0,1},{1,0},{2,3},{3,2},{4,5},{5,4},{6,7},{7,6},{8,9},{9,8},{10,11... | collective-permute-start | bytes 294920 | tf_op jit(solution)/shard_map/ppermute | solution.py:386
  31.7 0.8 collective-permute-done.3.border_ref
  32.6 8.0 %windows.1 = (bf16[4,8,16,192]{3,2,1,0:T(8,128)(2,1)S(1)}, bf16[4,8,8,192]{3,2,1,0:T(8,128)(2,1)S(1)}, f32[1536,128]{1,0:T(8,128)S(1)}) custom-call(s32[3]{0:T(128)S(1)} %add_convert_fusion.1.flags_ref, bf16[2,4,16,384]{3,2,1,0:T(8,128)(2,1)S(1)} %collective-permute-done.z_ref, bf16[2,4,16,384]{3,2,1,0:T(8,128)(2,1)S(1)} %collective-permute-done.1.zy_ref, ...), custom_call_target="tpu_custom_call" | custom-call | flops 1000000000 | bytes 3000000 | tf_op jit(solution)/shard_map/windows/pallas_call | solution.py:343
  40.6 2.3 %collective-permute-start.4 = (f32[768,128]{1,0:T(8,128)S(1)}, f32[768,128]{1,0:T(8,128)S(1)}, u32[]{:S(2)}, u32[]{:S(2)}) collective-permute-start(f32[768,128]{1,0:T(8,128)S(1)} %constant_dynamic-slice_fusion), channel_id=1, source_target_pairs={{0,1},{1,0},{2,3},{3,2},{4,5},{5,4},{6,7},{7,6},{8,9},{9,8},{10,11... | collective-permute-start | bytes 1179656 | tf_op jit(solution)/shard_map/ppermute | solution.py:411
  42.9 2.1 %collective-permute-start.5 = (bf16[4,8,8,192]{3,2,1,0:T(8,128)(2,1)S(1)}, bf16[4,8,8,192]{3,2,1,0:T(8,128)(2,1)S(1)}, u32[]{:S(2)}, u32[]{:S(2)}) collective-permute-start(bf16[4,8,8,192]{3,2,1,0:T(8,128)(2,1)S(1)} %get-tuple-element.30), channel_id=1, source_target_pairs={{0,1},{1,0},{2,3},{3,2},{4,5},{5,4},{6,7},{7,6},{8,9},{9,8},{10,11... | collective-permute-start | bytes 294920 | tf_op jit(solution)/shard_map/ppermute | solution.py:386
  45.0 1.2 %collective-permute-done.5 = bf16[4,8,8,192]{3,2,1,0:T(8,128)(2,1)S(1)} collective-permute-done((bf16[4,8,8,192]{3,2,1,0:T(8,128)(2,1)S(1)}, bf16[4,8,8,192]{3,2,1,0:T(8,128)(2,1)S(1)}, u32[]{:S(2)}, u32[]{:S(2)}) %collective-permute-start.5) | collective-permute-done | bytes 98336 | tf_op jit(solution)/shard_map/ppermute | solution.py:386
  46.2 0.7 add_convert_fusion
  46.9 7.3 %all-to-all-start = ((bf16[32,24,128]{2,1,0:T(8,128)(2,1)}), bf16[32,24,128]{2,1,0:T(8,128)(2,1)S(1)}, u32[]{:S(2)}, u32[]{:S(2)}) async-start(bf16[32,24,128]{2,1,0:T(8,128)(2,1)} %bitcast.10), calls=%async_computation | async-start | bytes 393216 | tf_op jit(solution)/shard_map/all_to_all | solution.py:434
  54.5 10.4 %all-to-all-done = bf16[32,24,128]{2,1,0:T(8,128)(2,1)S(1)} async-done(((bf16[32,24,128]{2,1,0:T(8,128)(2,1)}), bf16[32,24,128]{2,1,0:T(8,128)(2,1)S(1)}, u32[]{:S(2)}, u32[]{:S(2)}) %all-to-all-start) | async-done | bytes 196640 | tf_op jit(solution)/shard_map/all_to_all | solution.py:434
  64.9 0.6 broadcast_in_dim.4
  65.6 3.5 %all-to-all-start.1 = ((f32[8,24,128]{2,1,0:T(8,128)}), f32[8,24,128]{2,1,0:T(8,128)S(1)}, u32[]{:S(2)}, u32[]{:S(2)}) async-start(f32[8,24,128]{2,1,0:T(8,128)} %broadcast_in_dim.4), calls=%async_computation.1 | async-start | bytes 196608 | tf_op jit(solution)/shard_map/all_to_all | solution.py:417
  69.1 1.9 %collective-permute-start.6 = (bf16[4,4,16,192]{3,2,1,0:T(8,128)(2,1)S(1)}, bf16[4,4,16,192]{3,2,1,0:T(8,128)(2,1)S(1)}, u32[]{:S(2)}, u32[]{:S(2)}) collective-permute-start(bf16[4,4,16,192]{3,2,1,0:T(8,128)(2,1)S(1)} %fusion.4), channel_id=1, source_target_pairs={{0,2},{2,4},{4,6},{6,8},{8,10},{10,12},{12,14},{14,0},{1,3},{3,5},... | collective-permute-start | bytes 294920 | tf_op jit(solution)/shard_map/ppermute | solution.py:386
  71.0 5.6 %all-to-all-done.1 = f32[8,24,128]{2,1,0:T(8,128)S(1)} async-done(((f32[8,24,128]{2,1,0:T(8,128)}), f32[8,24,128]{2,1,0:T(8,128)S(1)}, u32[]{:S(2)}, u32[]{:S(2)}) %all-to-all-start.1) | async-done | bytes 98336 | tf_op jit(solution)/shard_map/all_to_all | solution.py:417
  76.6 0.5 collective-permute-done.6
  77.2 0.8 broadcast_in_dim.5
  77.9 3.9 %all-to-all-start.2 = ((f32[32,24,128]{2,1,0:T(8,128)}), f32[32,24,128]{2,1,0:T(8,128)S(1)}, u32[]{:S(2)}, u32[]{:S(2)}) async-start(f32[32,24,128]{2,1,0:T(8,128)} %broadcast_in_dim.5), calls=%async_computation.2 | async-start | bytes 786432 | tf_op jit(solution)/shard_map/all_to_all | solution.py:417
  81.9 3.1 %collective-permute-start.7 = (bf16[2,8,16,192]{3,2,1,0:T(8,128)(2,1)S(1)}, bf16[2,8,16,192]{3,2,1,0:T(8,128)(2,1)S(1)}, u32[]{:S(2)}, u32[]{:S(2)}) collective-permute-start(bf16[2,8,16,192]{3,2,1,0:T(8,128)(2,1)S(1)} %fusion.5), channel_id=1, source_target_pairs={{0,16},{16,32},{32,48},{48,64},{64,80},{80,96},{96,112},{112,128},... | collective-permute-start | bytes 294920 | tf_op jit(solution)/shard_map/ppermute | solution.py:386
  85.0 8.6 %all-to-all-done.2 = f32[32,24,128]{2,1,0:T(8,128)S(1)} async-done(((f32[32,24,128]{2,1,0:T(8,128)}), f32[32,24,128]{2,1,0:T(8,128)S(1)}, u32[]{:S(2)}, u32[]{:S(2)}) %all-to-all-start.2) | async-done | bytes 393248 | tf_op jit(solution)/shard_map/all_to_all | solution.py:417
  93.6 7.0 %all_gather.3.sums_ref = f32[1536,128]{1,0:T(8,128)S(1)} all-gather(f32[768,128]{1,0:T(8,128)S(1)} %bitcast.19), channel_id=1, replica_groups=mesh['yh'=4,'z'=8,'gy'=8,'gx'=2] {'gx'}, dimensions={0}, use_global_device_ids=true | all-gather | bytes 1179648 | tf_op jit(solution)/shard_map/all_gather | solution.py:442
  100.6 1.2 %finish.1 = (f32[192]{0:T(256)}, f32[192]{0:T(256)}, f32[192,576]{1,0:T(8,128)}, f32[576]{0:T(1024)}, f32[192,192]{1,0:T(8,128)}, /*index=5*/f32[6,1575]{1,0:T(8,128)}) custom-call(f32[1536,128]{1,0:T(8,128)S(1)} %all_gather.3.sums_ref), custom_call_target="tpu_custom_call" | custom-call | tf_op jit(solution)/shard_map/finish/pallas_call | solution.py:328
  101.8 0.8 fusion
  (39 shorter events, 1.7 us)
Async XLA Ops:
  1.9 26.1 %collective-permute-start = (bf16[2,4,16,384]{3,2,1,0:T(8,128)(2,1)S(1)}, bf16[2,4,16,384]{3,2,1,0:T(8,128)(2,1)S(1)}, u32[]{:S(2)}, u32[]{:S(2)}) collective-permute-start(bf16[2,4,16,384]{3,2,1,0:T(8,128)(2,1)S(1)} %get-tuple-element.52), channel_id=1, source_target_pairs={{0,496},{16,0},{32,16},{48,32},{64,48},{80,64},{96,80},{112,96},{1... | collective-permute-start | bytes 294920 | tf_op jit(solution)/shard_map/ppermute | solution.py:386
  17.1 7.0 %copy-start.5 = (f32[576]{0:T(1024)S(1)}, f32[576]{0:T(1024)}, u32[]{:S(2)}) copy-start(f32[576]{0:T(1024)} %param.12) | copy-start | bytes 6916
  17.1 11.0 %collective-permute-start.1 = (bf16[2,4,16,384]{3,2,1,0:T(8,128)(2,1)S(1)}, bf16[2,4,16,384]{3,2,1,0:T(8,128)(2,1)S(1)}, u32[]{:S(2)}, u32[]{:S(2)}) collective-permute-start(bf16[2,4,16,384]{3,2,1,0:T(8,128)(2,1)S(1)} %get-tuple-element.53), channel_id=1, source_target_pairs={{0,510},{2,496},{4,498},{6,500},{8,502},{10,504},{12,506},{14,508}... | collective-permute-start | bytes 294920 | tf_op jit(solution)/shard_map/ppermute | solution.py:386
  20.7 7.4 %collective-permute-start.2 = (bf16[2,4,16,384]{3,2,1,0:T(8,128)(2,1)S(1)}, bf16[2,4,16,384]{3,2,1,0:T(8,128)(2,1)S(1)}, u32[]{:S(2)}, u32[]{:S(2)}) collective-permute-start(bf16[2,4,16,384]{3,2,1,0:T(8,128)(2,1)S(1)} %get-tuple-element.54), channel_id=1, source_target_pairs={{0,14},{2,0},{4,2},{6,4},{8,6},{10,8},{12,10},{14,12},{1,15},{3,1}... | collective-permute-start | bytes 294920 | tf_op jit(solution)/shard_map/ppermute | solution.py:386
  24.1 0.8 copy-start.4
  25.8 1.0 copy-start.3
  27.1 0.7 copy-start.7
  27.1 1.0 copy-start.1
  27.1 1.0 copy-start.2
  27.3 0.7 copy-start.6
  28.1 4.4 %copy-start = (bf16[192,192]{1,0:T(8,128)(2,1)S(1)}, bf16[192,192]{1,0:T(8,128)(2,1)}, u32[]{:S(2)}) copy-start(bf16[192,192]{1,0:T(8,128)(2,1)} %proj_ref.1) | copy-start | bytes 221188
  28.2 4.4 %collective-permute-start.3 = (bf16[4,8,4,384]{3,2,1,0:T(4,128)(2,1)S(1)}, bf16[4,8,4,384]{3,2,1,0:T(4,128)(2,1)S(1)}, u32[]{:S(2)}, u32[]{:S(2)}) collective-permute-start(bf16[4,8,4,384]{3,2,1,0:T(4,128)(2,1)S(1)} %fusion.9), channel_id=1, source_target_pairs={{0,1},{1,0},{2,3},{3,2},{4,5},{5,4},{6,7},{7,6},{8,9},{9,8},{10,11... | collective-permute-start | bytes 294920 | tf_op jit(solution)/shard_map/ppermute | solution.py:386
  40.6 5.5 %collective-permute-start.4 = (f32[768,128]{1,0:T(8,128)S(1)}, f32[768,128]{1,0:T(8,128)S(1)}, u32[]{:S(2)}, u32[]{:S(2)}) collective-permute-start(f32[768,128]{1,0:T(8,128)S(1)} %constant_dynamic-slice_fusion), channel_id=1, source_target_pairs={{0,1},{1,0},{2,3},{3,2},{4,5},{5,4},{6,7},{7,6},{8,9},{9,8},{10,11... | collective-permute-start | bytes 1179656 | tf_op jit(solution)/shard_map/ppermute | solution.py:411
  42.9 3.2 %collective-permute-start.5 = (bf16[4,8,8,192]{3,2,1,0:T(8,128)(2,1)S(1)}, bf16[4,8,8,192]{3,2,1,0:T(8,128)(2,1)S(1)}, u32[]{:S(2)}, u32[]{:S(2)}) collective-permute-start(bf16[4,8,8,192]{3,2,1,0:T(8,128)(2,1)S(1)} %get-tuple-element.30), channel_id=1, source_target_pairs={{0,1},{1,0},{2,3},{3,2},{4,5},{5,4},{6,7},{7,6},{8,9},{9,8},{10,11... | collective-permute-start | bytes 294920 | tf_op jit(solution)/shard_map/ppermute | solution.py:386
  46.9 18.0 %all-to-all-start = ((bf16[32,24,128]{2,1,0:T(8,128)(2,1)}), bf16[32,24,128]{2,1,0:T(8,128)(2,1)S(1)}, u32[]{:S(2)}, u32[]{:S(2)}) async-start(bf16[32,24,128]{2,1,0:T(8,128)(2,1)} %bitcast.10), calls=%async_computation | async-start | bytes 393216 | tf_op jit(solution)/shard_map/all_to_all | solution.py:434
  65.6 11.0 %all-to-all-start.1 = ((f32[8,24,128]{2,1,0:T(8,128)}), f32[8,24,128]{2,1,0:T(8,128)S(1)}, u32[]{:S(2)}, u32[]{:S(2)}) async-start(f32[8,24,128]{2,1,0:T(8,128)} %broadcast_in_dim.4), calls=%async_computation.1 | async-start | bytes 196608 | tf_op jit(solution)/shard_map/all_to_all | solution.py:417
  69.1 8.1 %collective-permute-start.6 = (bf16[4,4,16,192]{3,2,1,0:T(8,128)(2,1)S(1)}, bf16[4,4,16,192]{3,2,1,0:T(8,128)(2,1)S(1)}, u32[]{:S(2)}, u32[]{:S(2)}) collective-permute-start(bf16[4,4,16,192]{3,2,1,0:T(8,128)(2,1)S(1)} %fusion.4), channel_id=1, source_target_pairs={{0,2},{2,4},{4,6},{6,8},{8,10},{10,12},{12,14},{14,0},{1,3},{3,5},... | collective-permute-start | bytes 294920 | tf_op jit(solution)/shard_map/ppermute | solution.py:386
  77.9 15.6 %all-to-all-start.2 = ((f32[32,24,128]{2,1,0:T(8,128)}), f32[32,24,128]{2,1,0:T(8,128)S(1)}, u32[]{:S(2)}, u32[]{:S(2)}) async-start(f32[32,24,128]{2,1,0:T(8,128)} %broadcast_in_dim.5), calls=%async_computation.2 | async-start | bytes 786432 | tf_op jit(solution)/shard_map/all_to_all | solution.py:417
  81.9 20.0 %collective-permute-start.7 = (bf16[2,8,16,192]{3,2,1,0:T(8,128)(2,1)S(1)}, bf16[2,8,16,192]{3,2,1,0:T(8,128)(2,1)S(1)}, u32[]{:S(2)}, u32[]{:S(2)}) collective-permute-start(bf16[2,8,16,192]{3,2,1,0:T(8,128)(2,1)S(1)} %fusion.5), channel_id=1, source_target_pairs={{0,16},{16,32},{32,48},{48,64},{64,80},{80,96},{96,112},{112,128},... | collective-permute-start | bytes 294920 | tf_op jit(solution)/shard_map/ppermute | solution.py:386
